TPU v7x, 32 devices: a whole 2x2x4 slice. The times are simulated.
32 devices in a mesh: row: 4 (over y, x), col: 8 (over z, core).
Axes of the slice: x: 2, y: 2, z: 4, core: 2. Of those that a mesh axis runs over, the one named last changes fastest.
Arguments:
- dofs: float32 [504, 8192], P(None, ('row', 'col')), may hold values from -6 to 6
- star: float32 [243, 8192], P(None, ('row', 'col')), may hold values from -1.25 to 1.25
- flux_mats: float32 [648, 8192], P(None, ('row', 'col')), may hold values from -0.75 to 0.75
- kxi: float32 [3, 56, 56], replicated, may hold values from -0.75 to 0.75
- face_proj: float32 [4, 56, 21], replicated, may hold values from -0.75 to 0.75
- face_lift: float32 [4, 21, 56], replicated, may hold values from -1.25 to 1.25
- orient: float32 [3, 21, 21], replicated, may hold values from -1.25 to 1.25
- neighbour: int32 [4, 8192], P(None, ('row', 'col')), may hold values from 0 to 2047
- orient_code: int32 [4, 8192], P(None, ('row', 'col')), may hold values from 0 to 2
- send_list: int32 [4, 2048], P(None, ('row', 'col')), may hold values from 0 to 255
- fault_part: int32 [4096, 1], P(('row', 'col')), may hold values from 0 to 31; in each aligned block of 128 rows (0 to 127, 128 to 255, ...) at most 8 rows name the same one
- fault_item: int32 [4096], P(('row', 'col')), may hold values from 0 to 1023
- shear_init: float32 [21, 4096], P(None, ('row', 'col')), may hold values from -8 to 8
- normal_init: float32 [21, 4096], P(None, ('row', 'col')), may hold values from 1 to 8
- state_var: float32 [21, 4096], P(None, ('row', 'col')), may hold values from 0.3 to 0.7
- slip_prev: float32 [21, 4096], P(None, ('row', 'col')), may hold values from 0.05 to 2
Outputs:
- dofs_next: float32 [504, 8192], P(None, ('row', 'col'))
- slip_rate: float32 [21, 4096], P(None, ('row', 'col'))
Inputs may be any that keep to these rules, and one draw needn't show every extreme that they name: `fault_part`: partitions are numbered r * 8 + c. Among the 128 fault rows held by one device, no partition is named by more than 8 rows.
All inputs are finite; a program needn't handle non-finite values.
Results may differ from a plain program's by a relative error of at most 0.0003.
Values sent between devices are 32-bit elements; how exact they have to be, the bound alone decides.
No kernel may reach another device: no remote copies, remote signals or barrier semaphores. Data moves between devices by JAX's collectives and lax.ppermute only.
A program may use at most 128 MiB of HBM per device.

v0:
```python
import jax
import jax.numpy as jnp
from jax import lax
from jax.experimental import pallas as pl
from jax.experimental.pallas import tpu as pltpu
from jax.sharding import PartitionSpec as P

QUANT = 9
ORDER = 6
NEWTON_ITERS = 3
FACES = 4
DIMS = 3
TURNS = 3

time_step = 2.0
fric_a = 0.5
f32 = jnp.float32
half = jnp.bfloat16
MIB = 2**20
LANES = 128
SUB = 8


def up(count, unit):
    return -(-count // unit) * unit


def inverse_sinh(value):
    magnitude = jnp.abs(value)
    squared = magnitude * magnitude
    positive = jnp.log1p(magnitude + squared / (1.0 + jnp.sqrt(1.0 + squared)))
    return jnp.where(value < 0.0, -positive, positive)


def friction_solve(shear, normal, shear_init, normal_init, state_var, slip_prev):
    shear_total = shear_init + shear
    normal_eff = normal_init * (1.0 + 0.5 * jnp.tanh(normal))
    growth = jnp.exp(state_var / fric_a) * 0.5
    slip_now = slip_prev
    for newton_step in range(NEWTON_ITERS):
        scaled = growth * slip_now
        misfit = shear_total - slip_now - fric_a * normal_eff * inverse_sinh(scaled)
        slope_val = -1.0 - fric_a * normal_eff * growth / jnp.sqrt(1.0 + scaled * scaled)
        slip_now = slip_now - misfit / slope_val
    return slip_now


def split(values):
    head = values.astype(half).astype(f32)
    return head, values - head


def pad_rows(values, rows):
    if values.shape[0] == rows:
        return values
    return jnp.concatenate(
        [values, jnp.zeros((rows - values.shape[0], values.shape[1]), f32)], axis=0
    )


def pad_lanes(values, lanes):
    if values.shape[1] == lanes:
        return values
    return jnp.concatenate(
        [values, jnp.zeros((values.shape[0], lanes - values.shape[1]), f32)], axis=1
    )


def pieces(values):
    head, rest = split(values)
    return pad_rows(jnp.concatenate([head, rest, head], axis=0), up(3 * values.shape[0], 16)).astype(
        half
    )


def table(values):
    head, rest = split(values)
    return pad_lanes(
        jnp.concatenate([head, head, rest], axis=1), up(3 * values.shape[1], 16)
    ).astype(half)


def product(left, right):
    return jnp.dot(left, right, preferred_element_type=f32)


def lane_row(ref, row, side):
    return ref[row : row + 1, side * LANES : (side + 1) * LANES]


def one_hot(first, rows, index_row):
    places = lax.broadcasted_iota(jnp.int32, (rows, index_row.shape[1]), 0) + first
    return jnp.where(places == index_row, 1.0, 0.0).astype(half)


def flat_row(ref):
    return jnp.concatenate([ref[i : i + 1, :] for i in range(ref.shape[0])], axis=1)


def star_apply(star_ref, moved_ref, basis, side, emit):
    group = 3
    for first in range(0, QUANT, group):
        totals = [None] * group
        for inner in range(QUANT):
            for axis_dir in range(DIMS):
                part = moved_ref[
                    inner,
                    axis_dir * basis : (axis_dir + 1) * basis,
                    side * LANES : (side + 1) * LANES,
                ]
                for i in range(group):
                    at = (axis_dir * QUANT + first + i) * QUANT + inner
                    term = lane_row(star_ref, at, side) * part
                    totals[i] = term if totals[i] is None else totals[i] + term
        for i in range(group):
            emit(first + i, totals[i])


def flux_apply(flux_ref, which, values_of, face, side, totals):
    for inner in range(QUANT):
        value = values_of(inner)
        for p in range(QUANT):
            at = ((face * 2 + which) * QUANT + p) * QUANT + inner
            term = lane_row(flux_ref, at, side) * value
            totals[p] = term if totals[p] is None else totals[p] + term
    return totals


def cost(flops, moved):
    return pl.CostEstimate(flops=flops, bytes_accessed=moved, transcendentals=0)


def call(kernel, name, outs, scratch=(), flops=0, moved=0):
    return pl.pallas_call(
        kernel,
        name=name,
        out_shape=outs,
        scratch_shapes=list(scratch),
        cost_estimate=cost(flops, moved),
        compiler_params=pltpu.CompilerParams(vmem_limit_bytes=48 * MIB),
    )


def per_device(
    dofs,
    star,
    flux_mats,
    kxi,
    face_proj,
    face_lift,
    orient,
    neighbour,
    orient_code,
    send_list,
    fault_part,
    fault_item,
    shear_init,
    normal_init,
    state_var,
    slip_prev,
):
    basis = kxi.shape[1]
    nodes = face_proj.shape[2]
    elems = dofs.shape[1]
    sides = elems // LANES
    ghosts = send_list.shape[1]
    ghost_all = 4 * ghosts
    node_pad = up(nodes, SUB)
    faults = fault_item.shape[0]
    devices = lax.axis_size("row") * lax.axis_size("col")
    slot_most = max(2, 2 * faults // devices)
    slots = devices * slot_most
    sides_all = FACES * elems
    left_q = (QUANT + 1) // 2
    depth = up(3 * basis, 16)
    turn_depth = up(3 * node_pad, 16)
    item_row = 4 * node_pad
    fault_rows = item_row + SUB

    def slot_kernel(part_ref, item_ref, shear_ref, normal_ref, state_ref, slip_ref, out_ref, slot_ref):
        by_row = lax.broadcasted_iota(jnp.int32, (faults, faults), 0)
        by_lane = lax.broadcasted_iota(jnp.int32, (faults, faults), 1)
        down = jnp.broadcast_to(part_ref[...], (faults, faults))
        across = jnp.sum(jnp.where(by_row == by_lane, down, 0), axis=0, keepdims=True)
        rank = jnp.sum(
            jnp.where((down == across) & (by_row < by_lane), 1, 0), axis=0, keepdims=True
        )
        place = across * slot_most + rank
        slot_ref[...] = place
        chosen = one_hot(0, slots, place)
        rows = [
            pad_rows(ref[...], node_pad) for ref in (shear_ref, normal_ref, state_ref, slip_ref)
        ]
        rows.append(pad_rows((item_ref[...] + 1).astype(f32), LANES - item_row))
        head, rest = split(jnp.concatenate(rows, axis=0))
        out_ref[...] = lax.dot_general(
            jnp.concatenate([chosen, chosen], axis=1),
            jnp.concatenate([head, rest], axis=1).astype(half),
            (((1,), (1,)), ((), ())),
            preferred_element_type=f32,
        )

    def predict_kernel(dofs_ref, star_ref, kxi_ref, send_ref, out_ref, *rest):
        sends, (moved_ref, piece_ref, table_ref) = rest[:4], rest[4:]
        table_ref[...] = table(jnp.concatenate([kxi_ref[d].T for d in range(DIMS)], axis=0))
        for q in range(QUANT):
            start = dofs_ref[q * basis : (q + 1) * basis, :]
            out_ref[q * basis : (q + 1) * basis, :] = time_step * start
            piece_ref[q] = pieces(start)

        def advance(order_k, factor):
            for q in range(QUANT):
                moved_ref[q] = product(table_ref[...], piece_ref[q])
            factor = factor * time_step / (order_k + 1).astype(f32)
            for side in range(sides):
                lanes = slice(side * LANES, (side + 1) * LANES)

                def emit(p, value):
                    piece_ref[p, :, lanes] = pieces(value)
                    rows = slice(p * basis, (p + 1) * basis)
                    out_ref[rows, lanes] = out_ref[rows, lanes] + factor * value

                star_apply(star_ref, moved_ref, basis, side, emit)
            return factor

        lax.fori_loop(1, ORDER, advance, f32(time_step))
        picks = send_ref[...]
        picks = jnp.concatenate([picks, picks], axis=1)
        width = 2 * ghosts
        chosen = jnp.concatenate(
            [one_hot(0, elems, picks[d : d + 1, :]) for d in range(4)], axis=1
        )
        low = lax.broadcasted_iota(jnp.int32, (basis, width), 1) < ghosts
        got = []
        for q in range(QUANT):
            head, rest_q = split(out_ref[q * basis : (q + 1) * basis, :])
            both = product(jnp.concatenate([head, rest_q], axis=0).astype(half), chosen)
            got.append(both[:basis] + both[basis:])
        for d in range(4):
            lanes = slice(d * width, (d + 1) * width)
            for q in range(left_q):
                first = got[q][:, lanes]
                second = got[q + left_q][:, lanes] if q + left_q < QUANT else first
                sends[d][q * basis : (q + 1) * basis, :] = jnp.where(low, first, second)

    def local_kernel(
        work_ref,
        dofs_ref,
        star_ref,
        flux_ref,
        kxi_ref,
        proj_ref,
        near_ref,
        base_ref,
        own_ref,
        fric_ref,
        seen_ref,
        moved_ref,
        trace_ref,
        piece_ref,
        left_ref,
        chosen_ref,
    ):
        turn_table = table(jnp.concatenate([kxi_ref[d] for d in range(DIMS)], axis=0))
        trace_table = table(
            jnp.concatenate([pad_rows(proj_ref[j].T, node_pad) for j in range(FACES)], axis=0)
        )
        both_table = jnp.concatenate([turn_table, trace_table], axis=0)
        turned = DIMS * basis
        for q in range(QUANT):
            got = product(both_table, pieces(work_ref[q * basis : (q + 1) * basis, :]))
            moved_ref[q] = got[:turned]
            trace_ref[q] = got[turned:]
            for j in range(FACES):
                head, rest = split(got[turned + j * node_pad : turned + (j + 1) * node_pad])
                left_ref[q * 2 * node_pad : (q + 1) * 2 * node_pad, j * elems : (j + 1) * elems] = (
                    jnp.concatenate([head, rest], axis=0).astype(half)
                )
        near = flat_row(near_ref)
        for j in range(FACES):
            chosen_ref[j * elems : (j + 1) * elems, :] = one_hot(j * elems, elems, near)
        seen_ref[...] = product(left_ref[...], chosen_ref[...]).astype(half)
        for j in range(FACES):
            rows = slice(j * node_pad, (j + 1) * node_pad)
            lanes = slice(j * elems, (j + 1) * elems)
            fric_ref[:node_pad, lanes] = 0.5 * (trace_ref[3, rows] + trace_ref[6, rows])
            fric_ref[node_pad:, lanes] = 0.5 * trace_ref[0, rows]
        for side in range(sides):
            lanes = slice(side * LANES, (side + 1) * LANES)

            def emit(p, value):
                rows = slice(p * basis, (p + 1) * basis)
                base_ref[rows, lanes] = dofs_ref[rows, lanes] + 0.25 * value

            star_apply(star_ref, moved_ref, basis, side, emit)
            for j in range(FACES):
                totals = flux_apply(
                    flux_ref,
                    0,
                    lambda q: trace_ref[q, j * node_pad : (j + 1) * node_pad, lanes],
                    j,
                    side,
                    [None] * QUANT,
                )
                for p in range(QUANT):
                    at = (j * QUANT + p) * node_pad
                    own_ref[at : at + node_pad, lanes] = totals[p]

    def ghost_kernel(
        got0_ref,
        got1_ref,
        got2_ref,
        got3_ref,
        proj_ref,
        orient_ref,
        near_ref,
        code_ref,
        seen_ref,
        fric_ref,
        asked_ref,
        turned_ref,
        slip_ref,
        back_ref,
        left_ref,
        chosen_ref,
    ):
        width = 2 * ghosts
        low = lax.broadcasted_iota(jnp.int32, (basis, width), 1) < ghosts
        trace_table = table(
            jnp.concatenate([pad_rows(proj_ref[j].T, node_pad) for j in range(FACES)], axis=0)
        )
        turn_table = table(
            jnp.concatenate(
                [pad_lanes(pad_rows(orient_ref[t].T, node_pad), node_pad) for t in range(TURNS)],
                axis=0,
            )
        )
        near = flat_row(near_ref)
        for j in range(FACES):
            chosen_ref[j * ghost_all : (j + 1) * ghost_all, :] = one_hot(
                sides_all + j * ghost_all, ghost_all, near
            )
        for q in range(QUANT):
            halves = []
            for first, second in ((got0_ref, got1_ref), (got2_ref, got3_ref)):
                if q < left_q:
                    rows = slice(q * basis, (q + 1) * basis)
                    a, b = first[rows, :], pltpu.roll(second[rows, :], ghosts, 1)
                else:
                    rows = slice((q - left_q) * basis, (q - left_q + 1) * basis)
                    a, b = pltpu.roll(first[rows, :], ghosts, 1), second[rows, :]
                halves.append(jnp.where(low, a, b))
            got = product(trace_table, pieces(jnp.concatenate(halves, axis=1)))
            for j in range(FACES):
                head, rest = split(got[j * node_pad : (j + 1) * node_pad])
                left_ref[
                    q * 2 * node_pad : (q + 1) * 2 * node_pad, j * ghost_all : (j + 1) * ghost_all
                ] = jnp.concatenate([head, rest], axis=0).astype(half)
        found = product(left_ref[...], chosen_ref[...]) + seen_ref[...].astype(f32)
        code = flat_row(code_ref)
        is_zero = jnp.broadcast_to(code, (node_pad, sides_all)) == 0
        is_one = jnp.broadcast_to(code, (node_pad, sides_all)) == 1
        kept = {}
        for q in range(QUANT):
            pair = found[q * 2 * node_pad : (q + 1) * 2 * node_pad]
            right = pad_rows(jnp.concatenate([pair, pair[:node_pad]], axis=0), turn_depth)
            rotated = product(turn_table, right.astype(half))
            value = jnp.where(
                is_zero,
                rotated[:node_pad],
                jnp.where(is_one, rotated[node_pad : 2 * node_pad], rotated[2 * node_pad :]),
            )
            turned_ref[q * node_pad : (q + 1) * node_pad, :] = value
            if q in (0, 3, 6):
                kept[q] = value
        shear = fric_ref[:node_pad, :] + 0.5 * (kept[3] - kept[6])
        normal = fric_ref[node_pad:, :] + 0.5 * kept[0]
        asked = asked_ref[...].T
        item = asked[item_row : item_row + 1, :].astype(jnp.int32) - 1
        wanted = one_hot(0, sides_all, item)
        shear_head, shear_rest = split(shear)
        normal_head, normal_rest = split(normal)
        taken = product(
            jnp.concatenate([shear_head, shear_rest, normal_head, normal_rest], axis=0).astype(half),
            wanted,
        )
        own = [asked[i * node_pad : (i + 1) * node_pad] for i in range(4)]
        slip = friction_solve(
            taken[:node_pad] + taken[node_pad : 2 * node_pad],
            taken[2 * node_pad : 3 * node_pad] + taken[3 * node_pad :],
            *own,
        )
        slip_ref[...] = slip
        back_ref[...] = pad_rows(slip, LANES).T

    def final_kernel(
        turned_ref, flux_ref, own_ref, base_ref, slip_ref, asked_ref, lift_ref, out_ref, mixed_ref
    ):
        lift_table = jnp.concatenate(
            [table(pad_lanes(lift_ref[j].T, node_pad)) for j in range(FACES)], axis=1
        )
        asked = asked_ref[...].T
        item = asked[item_row : item_row + 1, :].astype(jnp.int32) - 1
        wanted = one_hot(0, sides_all, item)
        slip_head, slip_rest = split(slip_ref[...])
        pushed = lax.dot_general(
            jnp.concatenate([slip_head, slip_rest], axis=0).astype(half),
            wanted,
            (((1,), (1,)), ((), ())),
            preferred_element_type=f32,
        )
        pushed = 2.0 * (pushed[:node_pad] + pushed[node_pad:])
        for side in range(sides):
            lanes = slice(side * LANES, (side + 1) * LANES)
            for j in range(FACES):
                at = j * elems + side * LANES
                rows_of = lambda p: slice((j * QUANT + p) * node_pad, (j * QUANT + p + 1) * node_pad)
                totals = [own_ref[rows_of(p), lanes] for p in range(QUANT)]
                push = pushed[:, at : at + LANES]
                totals[3] = totals[3] - push
                totals[6] = totals[6] + push
                totals = flux_apply(
                    flux_ref,
                    1,
                    lambda q: turned_ref[q * node_pad : (q + 1) * node_pad, at : at + LANES],
                    j,
                    side,
                    totals,
                )
                for p in range(QUANT):
                    mixed_ref[p, j * turn_depth : (j + 1) * turn_depth, lanes] = pieces(totals[p])
        for p in range(QUANT):
            rows = slice(p * basis, (p + 1) * basis)
            out_ref[rows, :] = base_ref[rows, :] + 0.25 * product(lift_table, mixed_ref[p])

    def return_kernel(slot_ref, back_ref, out_ref):
        chosen = one_hot(0, slots, slot_ref[...])
        head, rest = split(back_ref[...].T[:node_pad])
        got = product(jnp.concatenate([head, rest], axis=0).astype(half), chosen)
        out_ref[...] = (got[:node_pad] + got[node_pad:])[:nodes]

    shape = jax.ShapeDtypeStruct
    work_shape = shape(dofs.shape, f32)
    asked, slot_of = call(
        slot_kernel,
        "fault_slots",
        (shape((slots, LANES), f32), shape((1, faults), jnp.int32)),
        flops=2 * slots * 2 * faults * LANES,
        moved=400_000,
    )(fault_part, fault_item.reshape(1, faults), shear_init, normal_init, state_var, slip_prev)
    asked = lax.all_to_all(
        asked.reshape(devices, slot_most, LANES), ("row", "col"), split_axis=0, concat_axis=0, tiled=True
    ).reshape(slots, LANES)

    send_shape = shape((left_q * basis, 2 * ghosts), f32)
    work, *sends = call(
        predict_kernel,
        "predict",
        (work_shape,) + (send_shape,) * 4,
        scratch=(
            pltpu.VMEM((QUANT, DIMS * basis, elems), f32),
            pltpu.VMEM((QUANT, depth, elems), half),
            pltpu.VMEM((DIMS * basis, depth), half),
        ),
        flops=5 * 2 * DIMS * basis * depth * QUANT * elems,
        moved=8_000_000,
    )(dofs, star, kxi, send_list)

    def shifted(values, axis, step):
        count = lax.axis_size(axis)
        pairs = [(i, i + step) for i in range(count) if 0 <= i + step < count]
        return lax.ppermute(values, axis, pairs)

    from_low_row = shifted(sends[0], "row", 1)
    from_high_row = shifted(sends[1], "row", -1)
    from_low_col = shifted(sends[2], "col", 1)
    from_high_col = shifted(sends[3], "col", -1)

    base, own, fric, seen = call(
        local_kernel,
        "local_terms",
        (
            work_shape,
            shape((FACES * QUANT * node_pad, elems), f32),
            shape((2 * node_pad, sides_all), f32),
            shape((QUANT * 2 * node_pad, sides_all), half),
        ),
        scratch=(
            pltpu.VMEM((QUANT, DIMS * basis, elems), f32),
            pltpu.VMEM((QUANT, FACES * node_pad, elems), f32),
            pltpu.VMEM((QUANT, depth, elems), half),
            pltpu.VMEM((QUANT * 2 * node_pad, sides_all), half),
            pltpu.VMEM((sides_all, sides_all), half),
        ),
        flops=2 * QUANT * 2 * node_pad * sides_all * sides_all,
        moved=8_000_000,
    )(work, dofs, star, flux_mats, kxi, face_proj, neighbour)

    turned, slip, back = call(
        ghost_kernel,
        "ghost_terms",
        (
            shape((QUANT * node_pad, sides_all), f32),
            shape((node_pad, slots), f32),
            shape((slots, LANES), f32),
        ),
        scratch=(
            pltpu.VMEM((QUANT * 2 * node_pad, FACES * ghost_all), half),
            pltpu.VMEM((FACES * ghost_all, sides_all), half),
        ),
        flops=2 * QUANT * 2 * node_pad * sides_all * sides_all,
        moved=8_000_000,
    )(
        from_low_row,
        from_high_row,
        from_low_col,
        from_high_col,
        face_proj,
        orient,
        neighbour,
        orient_code,
        seen,
        fric,
        asked,
    )
    back = lax.all_to_all(
        back.reshape(devices, slot_most, LANES), ("row", "col"), split_axis=0, concat_axis=0, tiled=True
    ).reshape(slots, LANES)

    dofs_next = call(
        final_kernel,
        "final_terms",
        work_shape,
        scratch=(pltpu.VMEM((QUANT, FACES * turn_depth, elems), half),),
        flops=2 * QUANT * 2 * node_pad * sides_all * sides_all,
        moved=8_000_000,
    )(turned, flux_mats, own, base, slip, asked, face_lift)

    slip_rate = call(
        return_kernel,
        "fault_return",
        shape((nodes, faults), f32),
        flops=2 * 2 * node_pad * slots * faults,
        moved=200_000,
    )(slot_of, back)
    return dofs_next, slip_rate


def solution(mesh):
    across = ("row", "col")
    placed = (
        P(None, across),
        P(None, across),
        P(None, across),
        P(),
        P(),
        P(),
        P(),
        P(None, across),
        P(None, across),
        P(None, across),
        P(across, None),
        P(across),
        P(None, across),
        P(None, across),
        P(None, across),
        P(None, across),
    )
    return jax.shard_map(
        per_device,
        mesh=mesh,
        in_specs=placed,
        out_specs=(P(None, across), P(None, across)),
        check_vma=False,
    )
```

profile of v0, /device:TPU:0, one launch (start us, length us, event | category | flops | bytes accessed | tf_op | source)
XLA Modules:
  0.0 61.4 jit_solution(2190346377655189224)
XLA Ops:
  0.6 0.0 copy-start.1
  0.6 0.0 copy-start.2
  0.7 0.0 copy-start.3
  0.7 0.0 copy-start.4
  0.7 0.8 %copy.19.part_ref = s32[128,1]{1,0:T(8,128)S(1)} copy(s32[128,1]{0,1:T(1,128)} %param.26) | data formatting | bytes 1024 | tf_op args[10]
  1.5 0.0 copy-start.5
  1.5 0.0 copy-start.8
  1.5 0.0 copy-done.1
  1.5 0.0 copy-done.2
  1.5 0.0 copy-done.3
  1.5 0.0 copy-done.4
  1.5 0.6 copy-done.5
  2.1 0.9 %fault_slots.1 = (f32[256,128]{1,0:T(8,128)}, s32[1,128]{1,0:T(1,128)S(1)}) custom-call(s32[128,1]{1,0:T(8,128)S(1)} %copy.19.part_ref, s32[1,128]{1,0:T(1,128)S(1)} %bitcast.8, f32[21,128]{1,0:T(8,128)S(1)} %copy-done.1, f32[21,128]{1,0:T(8,128)S(1)} %copy-done.2, f32[21,128]{1,0:T(8,128)S(1)} %copy-done.3, f32[21,128]{1,0:T(8,128)S(1)} %copy-done.4), custom_call_target="tpu_custom_call" | custom-call | flops 16777216 | bytes 400000 | tf_op jit(solution)/shard_map/fault_slots/pallas_call | solution.py:444
  3.0 0.0 copy-start.9
  3.0 0.0 copy-start.13
  3.0 7.3 %all-to-all-start = ((f32[32,8,128]{2,1,0:T(8,128)}), f32[32,8,128]{2,1,0:T(8,128)S(1)}, u32[]{:S(2)}, u32[]{:S(2)}) async-start(f32[32,8,128]{2,1,0:T(8,128)} %bitcast.1), calls=%async_computation | async-start | bytes 262144 | tf_op jit(solution)/shard_map/all_to_all | solution.py:451
  10.3 0.0 copy-done.8
  10.3 0.0 copy-done.9
  10.3 0.0 copy-done.13
  10.4 0.0 copy-start.6
  10.4 1.0 %copy-done.6 = f32[504,256]{1,0:T(8,128)S(1)} copy-done((f32[504,256]{1,0:T(8,128)S(1)}, f32[504,256]{1,0:T(8,128)}, u32[]{:S(2)}) %copy-start.6) | copy-done | bytes 516120
  11.4 0.0 copy-start.20
  11.4 0.0 copy-start
  11.4 0.0 copy-start.7
  11.4 9.6 %predict.1 = (f32[504,256]{1,0:T(8,128)S(1)}, f32[280,128]{1,0:T(8,128)}, f32[280,128]{1,0:T(8,128)}, f32[280,128]{1,0:T(8,128)}, f32[280,128]{1,0:T(8,128)}) custom-call(f32[504,256]{1,0:T(8,128)S(1)} %copy-done.6, f32[243,256]{1,0:T(8,128)S(1)} %copy-done.8, f32[3,56,56]{2,1,0:T(8,128)S(1)} %copy-done.9, s32[4,64]{1,0:T(4,128)S(1)} %copy-done.13), custom_call_target="tpu_custom_call" | custom-call | flops 681246720 | bytes 8000000 | tf_op jit(solution)/shard_map/predict/pallas_call | solution.py:456
  21.0 0.0 copy-start.16
  21.0 0.8 %copy-done.16 = f32[504,256]{1,0:T(8,128)} copy-done((f32[504,256]{1,0:T(8,128)}, f32[504,256]{1,0:T(8,128)S(1)}, u32[]{:S(2)}) %copy-start.16) | copy-done | bytes 516120
  21.8 3.7 %collective-permute-start = (f32[280,128]{1,0:T(8,128)}, f32[280,128]{1,0:T(8,128)S(1)}, u32[]{:S(2)}, u32[]{:S(2)}) collective-permute-start(f32[280,128]{1,0:T(8,128)} %get-tuple-element.16), channel_id=1, source_target_pairs={{0,8},{8,16},{16,24},{1,9},{9,17},{17,25},{2,10},{10,18},{18,26},{... | collective-permute-start | bytes 430088 | tf_op jit(solution)/shard_map/ppermute | solution.py:472
  25.4 1.3 %collective-permute-start.1 = (f32[280,128]{1,0:T(8,128)}, f32[280,128]{1,0:T(8,128)S(1)}, u32[]{:S(2)}, u32[]{:S(2)}) collective-permute-start(f32[280,128]{1,0:T(8,128)} %get-tuple-element.17), channel_id=1, source_target_pairs={{8,0},{16,8},{24,16},{9,1},{17,9},{25,17},{10,2},{18,10},{26,18},{... | collective-permute-start | bytes 430088 | tf_op jit(solution)/shard_map/ppermute | solution.py:472
  26.7 2.4 %collective-permute-start.2 = (f32[280,128]{1,0:T(8,128)}, f32[280,128]{1,0:T(8,128)}, u32[]{:S(2)}, u32[]{:S(2)}) collective-permute-start(f32[280,128]{1,0:T(8,128)} %get-tuple-element.18), channel_id=1, source_target_pairs={{0,1},{1,2},{2,3},{3,4},{4,5},{5,6},{6,7},{8,9},{9,10},{10,11},{11... | collective-permute-start | bytes 430088 | tf_op jit(solution)/shard_map/ppermute | solution.py:472
  29.2 0.0 copy-start.11
  29.2 1.4 %collective-permute-start.3 = (f32[280,128]{1,0:T(8,128)}, f32[280,128]{1,0:T(8,128)}, u32[]{:S(2)}, u32[]{:S(2)}) collective-permute-start(f32[280,128]{1,0:T(8,128)} %get-tuple-element.19), channel_id=1, source_target_pairs={{1,0},{2,1},{3,2},{4,3},{5,4},{6,5},{7,6},{9,8},{10,9},{11,10},{12... | collective-permute-start | bytes 430088 | tf_op jit(solution)/shard_map/ppermute | solution.py:472
  30.6 0.0 copy-done.20
  30.6 0.1 copy.20.proj_ref
  30.7 0.0 copy-done
  30.7 0.0 copy-done.7
  30.7 0.0 copy-done.11
  30.7 0.0 copy-start.17
  30.8 1.0 %copy-done.17 = f32[504,256]{1,0:T(8,128)S(1)} copy-done((f32[504,256]{1,0:T(8,128)S(1)}, f32[504,256]{1,0:T(8,128)}, u32[]{:S(2)}) %copy-start.17) | copy-done | bytes 516120
  31.8 3.2 %local_terms.1 = (f32[504,256]{1,0:T(8,128)S(1)}, f32[864,256]{1,0:T(8,128)S(1)}, f32[48,1024]{1,0:T(8,128)S(1)}, bf16[432,1024]{1,0:T(8,128)(2,1)S(1)}) custom-call(f32[504,256]{1,0:T(8,128)S(1)} %copy-done.17, f32[504,256]{1,0:T(8,128)S(1)} %copy-done.7, f32[243,256]{1,0:T(8,128)S(1)} %copy-done.8, f32[648,256]{1,0:T(8,128)S(1)} %copy-done, ...), custom_call_target="tpu_custom_call" | custom-call | flops 905969664 | bytes 8000000 | tf_op jit(solution)/shard_map/local_terms/pallas_call | solution.py:479
  35.0 0.0 copy-start.14
  35.0 0.9 %copy-done.14 = bf16[432,1024]{1,0:T(8,128)(2,1)} copy-done((bf16[432,1024]{1,0:T(8,128)(2,1)}, bf16[432,1024]{1,0:T(8,128)(2,1)S(1)}, u32[]{:S(2)}) %copy-start.14) | copy-done | bytes 884760
  35.9 0.0 copy-start.18
  35.9 0.7 %copy-done.18 = f32[48,1024]{1,0:T(8,128)} copy-done((f32[48,1024]{1,0:T(8,128)}, f32[48,1024]{1,0:T(8,128)S(1)}, u32[]{:S(2)}) %copy-start.18) | copy-done | bytes 196632
  36.6 0.0 copy-start.12
  36.6 0.0 collective-permute-done.got0_ref
  36.6 0.0 collective-permute-done.1.got1_ref
  36.6 0.0 collective-permute-done.2.got2_ref
  36.6 0.0 collective-permute-done.3.got3_ref
  36.6 0.0 all-to-all-done
  36.6 0.6 %copy-done.12 = s32[4,256]{1,0:T(4,128)S(1)} copy-done((s32[4,256]{1,0:T(4,128)S(1)}, s32[4,256]{1,0:T(4,128)}, u32[]{:S(2)}) %copy-start.12) | copy-done | bytes 4120
  37.3 0.0 copy-start.10
  37.3 0.8 %copy-done.10 = f32[3,21,21]{2,1,0:T(8,128)S(1)} copy-done((f32[3,21,21]{2,1,0:T(8,128)S(1)}, f32[3,21,21]{2,1,0:T(8,128)}, u32[]{:S(2)}) %copy-start.10) | copy-done | bytes 5316
  38.0 0.0 copy-start.15
  38.0 1.2 %copy-done.15 = bf16[432,1024]{1,0:T(8,128)(2,1)S(1)} copy-done((bf16[432,1024]{1,0:T(8,128)(2,1)S(1)}, bf16[432,1024]{1,0:T(8,128)(2,1)}, u32[]{:S(2)}) %copy-start.15) | copy-done | bytes 884760
  39.2 0.0 copy-start.19
  39.2 0.9 %copy-done.19 = f32[48,1024]{1,0:T(8,128)S(1)} copy-done((f32[48,1024]{1,0:T(8,128)S(1)}, f32[48,1024]{1,0:T(8,128)}, u32[]{:S(2)}) %copy-start.19) | copy-done | bytes 196632
  40.1 3.8 %ghost_terms.1 = (f32[216,1024]{1,0:T(8,128)S(1)}, f32[24,256]{1,0:T(8,128)S(1)}, f32[256,128]{1,0:T(8,128)}) custom-call(f32[280,128]{1,0:T(8,128)S(1)} %collective-permute-done.got0_ref, f32[280,128]{1,0:T(8,128)S(1)} %collective-permute-done.1.got1_ref, f32[280,128]{1,0:T(8,128)} %collective-permute-done.2.got2_ref, ...), custom_call_target="tpu_custom_call" | custom-call | flops 905969664 | bytes 8000000 | tf_op jit(solution)/shard_map/ghost_terms/pallas_call | solution.py:499
  44.0 0.0 copy-start.21
  44.0 8.4 %all-to-all-start.1 = ((f32[32,8,128]{2,1,0:T(8,128)}), f32[32,8,128]{2,1,0:T(8,128)S(1)}, u32[]{:S(2)}, u32[]{:S(2)}) async-start(f32[32,8,128]{2,1,0:T(8,128)} %bitcast.3), calls=%async_computation.1 | async-start | bytes 262144 | tf_op jit(solution)/shard_map/all_to_all | solution.py:526
  52.4 0.0 copy-done.21
  52.4 2.2 %final_terms.1 = f32[504,256]{1,0:T(8,128)} custom-call(f32[216,1024]{1,0:T(8,128)S(1)} %get-tuple-element.24.turned_ref, f32[648,256]{1,0:T(8,128)S(1)} %copy-done, f32[864,256]{1,0:T(8,128)S(1)} %get-tuple-element.25.own_ref, f32[504,256]{1,0:T(8,128)S(1)} %get-tuple-element.26.base_ref, f32[24,256]{1,0:T(8,128)S(1)} %get-tuple-element.27.slip_ref, ...), custom_call_target="tpu_custom_call" | custom-call | flops 905969664 | bytes 8000000 | tf_op jit(solution)/shard_map/final_terms/pallas_call | solution.py:530
  54.6 6.0 %all-to-all-done.1 = f32[32,8,128]{2,1,0:T(8,128)S(1)} async-done(((f32[32,8,128]{2,1,0:T(8,128)}), f32[32,8,128]{2,1,0:T(8,128)S(1)}, u32[]{:S(2)}, u32[]{:S(2)}) %all-to-all-start.1) | async-done | bytes 131104 | tf_op jit(solution)/shard_map/all_to_all | solution.py:526
  60.6 0.8 %fault_return.1 = f32[21,128]{1,0:T(8,128)} custom-call(s32[1,128]{1,0:T(1,128)S(1)} %get-tuple-element.28.slot_ref, f32[256,128]{1,0:T(8,128)S(1)} %bitcast.7), custom_call_target="tpu_custom_call" | custom-call | flops 3145728 | bytes 200000 | tf_op jit(solution)/shard_map/fault_return/pallas_call | solution.py:539
  (1 shorter events, 0.0 us)
Async XLA Ops:
  0.6 0.8 %copy-start.1 = (f32[21,128]{1,0:T(8,128)S(1)}, f32[21,128]{1,0:T(8,128)}, u32[]{:S(2)}) copy-start(f32[21,128]{1,0:T(8,128)} %shear_ref.1) | copy-start | bytes 32260
  0.6 0.8 %copy-start.2 = (f32[21,128]{1,0:T(8,128)S(1)}, f32[21,128]{1,0:T(8,128)}, u32[]{:S(2)}) copy-start(f32[21,128]{1,0:T(8,128)} %normal_ref.1) | copy-start | bytes 32260
  0.7 0.8 %copy-start.3 = (f32[21,128]{1,0:T(8,128)S(1)}, f32[21,128]{1,0:T(8,128)}, u32[]{:S(2)}) copy-start(f32[21,128]{1,0:T(8,128)} %state_ref.1) | copy-start | bytes 32260
  0.7 0.8 %copy-start.4 = (f32[21,128]{1,0:T(8,128)S(1)}, f32[21,128]{1,0:T(8,128)}, u32[]{:S(2)}) copy-start(f32[21,128]{1,0:T(8,128)} %slip_ref.1) | copy-start | bytes 32260
  1.5 0.7 %copy-start.5 = (s32[128]{0:T(128)S(1)}, s32[128]{0:T(128)}, u32[]{:S(2)}) copy-start(s32[128]{0:T(128)} %param.27) | copy-start | bytes 1540
  1.5 8.9 %copy-start.8 = (f32[243,256]{1,0:T(8,128)S(1)}, f32[243,256]{1,0:T(8,128)}, u32[]{:S(2)}) copy-start(f32[243,256]{1,0:T(8,128)} %star_ref.3) | copy-start | bytes 746500
  3.0 7.3 %copy-start.9 = (f32[3,56,56]{2,1,0:T(8,128)S(1)}, f32[3,56,56]{2,1,0:T(8,128)}, u32[]{:S(2)}) copy-start(f32[3,56,56]{2,1,0:T(8,128)} %kxi_ref.3) | copy-start | bytes 112900
  3.0 7.3 %copy-start.13 = (s32[4,64]{1,0:T(4,128)S(1)}, s32[4,64]{1,0:T(4,128)}, u32[]{:S(2)}) copy-start(s32[4,64]{1,0:T(4,128)} %send_ref.1) | copy-start | bytes 3076
  3.0 33.6 %all-to-all-start = ((f32[32,8,128]{2,1,0:T(8,128)}), f32[32,8,128]{2,1,0:T(8,128)S(1)}, u32[]{:S(2)}, u32[]{:S(2)}) async-start(f32[32,8,128]{2,1,0:T(8,128)} %bitcast.1), calls=%async_computation | async-start | bytes 262144 | tf_op jit(solution)/shard_map/all_to_all | solution.py:451
  10.4 1.0 %copy-start.6 = (f32[504,256]{1,0:T(8,128)S(1)}, f32[504,256]{1,0:T(8,128)}, u32[]{:S(2)}) copy-start(f32[504,256]{1,0:T(8,128)} %dofs_ref.3) | copy-start | bytes 1548292
  11.4 19.2 %copy-start.20 = (f32[4,56,21]{1,0,2:T(4,128)S(1)}, f32[4,56,21]{1,0,2:T(4,128)}, u32[]{:S(2)}) copy-start(f32[4,56,21]{1,0,2:T(4,128)} %param.20) | copy-start | bytes 56452
  11.4 19.3 %copy-start = (f32[648,256]{1,0:T(8,128)S(1)}, f32[648,256]{1,0:T(8,128)}, u32[]{:S(2)}) copy-start(f32[648,256]{1,0:T(8,128)} %flux_ref.3) | copy-start | bytes 1990660
  11.4 19.3 %copy-start.7 = (f32[504,256]{1,0:T(8,128)S(1)}, f32[504,256]{1,0:T(8,128)}, u32[]{:S(2)}) copy-start(f32[504,256]{1,0:T(8,128)} %dofs_ref.3) | copy-start | bytes 1548292
  21.0 0.8 %copy-start.16 = (f32[504,256]{1,0:T(8,128)}, f32[504,256]{1,0:T(8,128)S(1)}, u32[]{:S(2)}) copy-start(f32[504,256]{1,0:T(8,128)S(1)} %get-tuple-element.20.work_ref) | copy-start | bytes 1548292
  21.8 14.8 %collective-permute-start = (f32[280,128]{1,0:T(8,128)}, f32[280,128]{1,0:T(8,128)S(1)}, u32[]{:S(2)}, u32[]{:S(2)}) collective-permute-start(f32[280,128]{1,0:T(8,128)} %get-tuple-element.16), channel_id=1, source_target_pairs={{0,8},{8,16},{16,24},{1,9},{9,17},{17,25},{2,10},{10,18},{18,26},{... | collective-permute-start | bytes 430088 | tf_op jit(solution)/shard_map/ppermute | solution.py:472
  25.4 11.2 %collective-permute-start.1 = (f32[280,128]{1,0:T(8,128)}, f32[280,128]{1,0:T(8,128)S(1)}, u32[]{:S(2)}, u32[]{:S(2)}) collective-permute-start(f32[280,128]{1,0:T(8,128)} %get-tuple-element.17), channel_id=1, source_target_pairs={{8,0},{16,8},{24,16},{9,1},{17,9},{25,17},{10,2},{18,10},{26,18},{... | collective-permute-start | bytes 430088 | tf_op jit(solution)/shard_map/ppermute | solution.py:472
  26.7 9.9 %collective-permute-start.2 = (f32[280,128]{1,0:T(8,128)}, f32[280,128]{1,0:T(8,128)}, u32[]{:S(2)}, u32[]{:S(2)}) collective-permute-start(f32[280,128]{1,0:T(8,128)} %get-tuple-element.18), channel_id=1, source_target_pairs={{0,1},{1,2},{2,3},{3,4},{4,5},{5,6},{6,7},{8,9},{9,10},{10,11},{11... | collective-permute-start | bytes 430088 | tf_op jit(solution)/shard_map/ppermute | solution.py:472
  29.2 1.6 %copy-start.11 = (s32[4,256]{1,0:T(4,128)S(1)}, s32[4,256]{1,0:T(4,128)}, u32[]{:S(2)}) copy-start(s32[4,256]{1,0:T(4,128)} %near_ref.3) | copy-start | bytes 12292
  29.2 7.4 %collective-permute-start.3 = (f32[280,128]{1,0:T(8,128)}, f32[280,128]{1,0:T(8,128)}, u32[]{:S(2)}, u32[]{:S(2)}) collective-permute-start(f32[280,128]{1,0:T(8,128)} %get-tuple-element.19), channel_id=1, source_target_pairs={{1,0},{2,1},{3,2},{4,3},{5,4},{6,5},{7,6},{9,8},{10,9},{11,10},{12... | collective-permute-start | bytes 430088 | tf_op jit(solution)/shard_map/ppermute | solution.py:472
  30.7 1.0 %copy-start.17 = (f32[504,256]{1,0:T(8,128)S(1)}, f32[504,256]{1,0:T(8,128)}, u32[]{:S(2)}) copy-start(f32[504,256]{1,0:T(8,128)} %copy-done.16) | copy-start | bytes 1548292
  35.0 0.9 %copy-start.14 = (bf16[432,1024]{1,0:T(8,128)(2,1)}, bf16[432,1024]{1,0:T(8,128)(2,1)S(1)}, u32[]{:S(2)}) copy-start(bf16[432,1024]{1,0:T(8,128)(2,1)S(1)} %get-tuple-element.21.seen_ref) | copy-start | bytes 2654212
  35.9 0.7 %copy-start.18 = (f32[48,1024]{1,0:T(8,128)}, f32[48,1024]{1,0:T(8,128)S(1)}, u32[]{:S(2)}) copy-start(f32[48,1024]{1,0:T(8,128)S(1)} %get-tuple-element.22.fric_ref) | copy-start | bytes 589828
  36.6 0.7 %copy-start.12 = (s32[4,256]{1,0:T(4,128)S(1)}, s32[4,256]{1,0:T(4,128)}, u32[]{:S(2)}) copy-start(s32[4,256]{1,0:T(4,128)} %code_ref.1) | copy-start | bytes 12292
  37.3 0.8 %copy-start.10 = (f32[3,21,21]{2,1,0:T(8,128)S(1)}, f32[3,21,21]{2,1,0:T(8,128)}, u32[]{:S(2)}) copy-start(f32[3,21,21]{2,1,0:T(8,128)} %orient_ref.1) | copy-start | bytes 15880
  38.0 1.2 %copy-start.15 = (bf16[432,1024]{1,0:T(8,128)(2,1)S(1)}, bf16[432,1024]{1,0:T(8,128)(2,1)}, u32[]{:S(2)}) copy-start(bf16[432,1024]{1,0:T(8,128)(2,1)} %copy-done.14) | copy-start | bytes 2654212
  39.2 0.9 %copy-start.19 = (f32[48,1024]{1,0:T(8,128)S(1)}, f32[48,1024]{1,0:T(8,128)}, u32[]{:S(2)}) copy-start(f32[48,1024]{1,0:T(8,128)} %copy-done.18) | copy-start | bytes 589828
  44.0 8.4 %copy-start.21 = (f32[4,21,56]{2,0,1:T(4,128)S(1)}, f32[4,21,56]{2,0,1:T(4,128)}, u32[]{:S(2)}) copy-start(f32[4,21,56]{2,0,1:T(4,128)} %param.21) | copy-start | bytes 56452
  44.0 16.6 %all-to-all-start.1 = ((f32[32,8,128]{2,1,0:T(8,128)}), f32[32,8,128]{2,1,0:T(8,128)S(1)}, u32[]{:S(2)}, u32[]{:S(2)}) async-start(f32[32,8,128]{2,1,0:T(8,128)} %bitcast.3), calls=%async_computation.1 | async-start | bytes 262144 | tf_op jit(solution)/shard_map/all_to_all | solution.py:526
where the time goes:
time: 62.1 us; the launch traced here: 61.4 us
  starting transfers between devices  24.5 us (39%)
  Pallas kernels  20.4 us (33%)
  local copies, waits for them, and re-layouts  9.49 us (15%)
  waiting for transfers between devices  6.01 us (10%)
  between operations  0.89 us (1%)
    pallas_call x1, Pallas kernels, per_device(): call(predict_kernel, 'predict', (work_shape,) + (send_shape,) * 4, scratc...  9.56 us
    unnamed x47, local copies, waits for them, and re-layouts  9.49 us
    ppermute x4, starting transfers between devices, shifted(): return lax.ppermute(values, axis, pairs)  8.82 us
    all_to_all x1, starting transfers between devices, per_device(): lax.all_to_all(back.reshape(devices, slot_most, LANES), ('row', 'col'), s...  8.43 us
    all_to_all x1, starting transfers between devices, per_device(): lax.all_to_all(asked.reshape(devices, slot_most, LANES), ('row', 'col'),...  7.3 us
    all_to_all x1, waiting for transfers between devices, per_device(): lax.all_to_all(back.reshape(devices, slot_most, LANES), ('row', 'col'), s...  6 us
    pallas_call x1, Pallas kernels, per_device(): call(ghost_kernel, 'ghost_terms', (shape((QUANT * node_pad, sides_all), f...  3.83 us
    pallas_call x1, Pallas kernels, per_device(): call(local_kernel, 'local_terms', (work_shape, shape((FACES * QUANT * nod...  3.2 us
  transfers between devices with their start and end apart: 6, of which 1 were waited for; matrix products, arithmetic and copies ran while one was open for 0% of the time, Pallas kernels for 24%

commit v1 on v0

v1 whole, which is shorter than its diff:
```python
import jax
import jax.numpy as jnp
from jax import lax
from jax.experimental import pallas as pl
from jax.experimental.pallas import tpu as pltpu
from jax.sharding import PartitionSpec as P

QUANT = 9
ORDER = 6
NEWTON_ITERS = 3
FACES = 4
DIMS = 3
TURNS = 3

time_step = 2.0
fric_a = 0.5
f32 = jnp.float32
half = jnp.bfloat16
MIB = 2**20
LANES = 128
SUB = 8


def up(count, unit):
    return -(-count // unit) * unit


def inverse_sinh(value):
    magnitude = jnp.abs(value)
    squared = magnitude * magnitude
    positive = jnp.log1p(magnitude + squared / (1.0 + jnp.sqrt(1.0 + squared)))
    return jnp.where(value < 0.0, -positive, positive)


def friction_solve(shear, normal, shear_init, normal_init, state_var, slip_prev):
    shear_total = shear_init + shear
    normal_eff = normal_init * (1.0 + 0.5 * jnp.tanh(normal))
    growth = jnp.exp(state_var / fric_a) * 0.5
    slip_now = slip_prev
    for newton_step in range(NEWTON_ITERS):
        scaled = growth * slip_now
        misfit = shear_total - slip_now - fric_a * normal_eff * inverse_sinh(scaled)
        slope_val = -1.0 - fric_a * normal_eff * growth / jnp.sqrt(1.0 + scaled * scaled)
        slip_now = slip_now - misfit / slope_val
    return slip_now


def split(values):
    head = values.astype(half).astype(f32)
    return head, values - head


def pad_rows(values, rows):
    if values.shape[0] == rows:
        return values
    return jnp.concatenate(
        [values, jnp.zeros((rows - values.shape[0], values.shape[1]), f32)], axis=0
    )


def pad_lanes(values, lanes):
    if values.shape[1] == lanes:
        return values
    return jnp.concatenate(
        [values, jnp.zeros((values.shape[0], lanes - values.shape[1]), f32)], axis=1
    )


def pieces(values):
    head, rest = split(values)
    return pad_rows(jnp.concatenate([head, rest, head], axis=0), up(3 * values.shape[0], 16)).astype(
        half
    )


def table(values):
    head, rest = split(values)
    return pad_lanes(
        jnp.concatenate([head, head, rest], axis=1), up(3 * values.shape[1], 16)
    ).astype(half)


def product(left, right):
    return jnp.dot(left, right, preferred_element_type=f32)


def lane_row(ref, row, side):
    return ref[row : row + 1, side * LANES : (side + 1) * LANES]


def one_hot(first, rows, index_row):
    places = lax.broadcasted_iota(jnp.int32, (rows, index_row.shape[1]), 0) + first
    return jnp.where(places == index_row, 1.0, 0.0).astype(half)


def flat_row(ref):
    return jnp.concatenate([ref[i : i + 1, :] for i in range(ref.shape[0])], axis=1)


def star_apply(star_ref, moved_ref, basis, side, emit):
    group = 3
    for first in range(0, QUANT, group):
        totals = [None] * group
        for inner in range(QUANT):
            for axis_dir in range(DIMS):
                part = moved_ref[
                    inner,
                    axis_dir * basis : (axis_dir + 1) * basis,
                    side * LANES : (side + 1) * LANES,
                ]
                for i in range(group):
                    at = (axis_dir * QUANT + first + i) * QUANT + inner
                    term = lane_row(star_ref, at, side) * part
                    totals[i] = term if totals[i] is None else totals[i] + term
        for i in range(group):
            emit(first + i, totals[i])


def flux_apply(flux_ref, which, values_of, face, side, totals):
    for inner in range(QUANT):
        value = values_of(inner)
        for p in range(QUANT):
            at = ((face * 2 + which) * QUANT + p) * QUANT + inner
            term = lane_row(flux_ref, at, side) * value
            totals[p] = term if totals[p] is None else totals[p] + term
    return totals


class Kept:
    def __init__(self, array):
        self.array = array


class Left:
    def __init__(self, array):
        self.array = array


class Inputs:
    def __init__(self, sources, targets, sems):
        self.sources, self.targets, self.waiting = sources, targets, {}
        for i, (source, target) in enumerate(zip(sources, targets)):
            if source is target:
                continue
            self.waiting[i] = pltpu.make_async_copy(source, target, sems.at[i])
            self.waiting[i].start()

    def __getitem__(self, i):
        if i in self.waiting:
            self.waiting.pop(i).wait()
        return self.targets[i]

    def rest(self):
        for move in self.waiting.values():
            move.wait()


class Outputs:
    def __init__(self, targets, sources, sems):
        self.targets, self.sources, self.sems = targets, sources, sems
        self.moving = []

    def __getitem__(self, i):
        return self.targets[i] if self.sources[i] is None else self.sources[i]

    def flush(self, i, rows=None):
        source, target = self.sources[i], self.targets[i]
        if source is None:
            return
        if rows is not None:
            source, target = source.at[rows], target.at[rows]
        move = pltpu.make_async_copy(source, target, self.sems.at[len(self.moving)])
        move.start()
        self.moving.append(move)

    def wait(self):
        for move in self.moving:
            move.wait()


def call(kernel, name, ins, outs, scratch=(), flops=0, moved=0, room=32, flushes=None):
    n_in, n_out = len(ins), len(outs)
    placed = [i for i, one in enumerate(outs) if one[2] == "hbm"]
    stays = [isinstance(one, Kept) for one in ins]
    brought = [i for i in range(n_in) if not isinstance(ins[i], (Kept, Left))]
    ins = [one.array if isinstance(one, (Kept, Left)) else one for one in ins]
    flushes = flushes or max(1, len(placed))

    def body(*refs):
        sources, targets = refs[:n_in], refs[n_in : n_in + n_out]
        at = n_in + n_out
        held = list(sources)
        for i in brought:
            held[i], at = refs[at], at + 1
        kept, at = refs[at : at + len(placed)], at + len(placed)
        in_sems, out_sems, *more = refs[at:]
        source_of = [None] * n_out
        for i, ref in zip(placed, kept):
            source_of[i] = ref
        inputs = Inputs(sources, held, in_sems)
        outputs = Outputs(targets, source_of, out_sems)
        kernel(inputs, outputs, *more)
        inputs.rest()
        outputs.wait()

    shapes = [
        {"hbm": pltpu.HBM, "vmem": pltpu.VMEM, "any": jax.ShapeDtypeStruct}[one[2]](one[0], one[1])
        for one in outs
    ]
    spaces = [pltpu.VMEM if one else pltpu.HBM for one in stays]
    return pl.pallas_call(
        body,
        name=name,
        out_shape=shapes,
        in_specs=[pl.BlockSpec(memory_space=space) for space in spaces],
        scratch_shapes=[
            *(pltpu.VMEM(ins[i].shape, ins[i].dtype) for i in brought),
            *(pltpu.VMEM(outs[i][0], outs[i][1]) for i in placed),
            pltpu.SemaphoreType.DMA((max(1, n_in),)),
            pltpu.SemaphoreType.DMA((flushes,)),
            *scratch,
        ],
        cost_estimate=pl.CostEstimate(flops=flops, bytes_accessed=moved, transcendentals=0),
        compiler_params=pltpu.CompilerParams(vmem_limit_bytes=room * MIB),
    )(*(pltpu.with_memory_space_constraint(a, space) for a, space in zip(ins, spaces)))


def per_device(
    dofs,
    star,
    flux_mats,
    kxi,
    face_proj,
    face_lift,
    orient,
    neighbour,
    orient_code,
    send_list,
    fault_part,
    fault_item,
    shear_init,
    normal_init,
    state_var,
    slip_prev,
):
    basis = kxi.shape[1]
    nodes = face_proj.shape[2]
    elems = dofs.shape[1]
    sides = elems // LANES
    ghosts = send_list.shape[1]
    ghost_all = 4 * ghosts
    node_pad = up(nodes, SUB)
    faults = fault_item.shape[0]
    devices = lax.axis_size("row") * lax.axis_size("col")
    slot_most = max(2, 2 * faults // devices)
    slots = devices * slot_most
    sides_all = FACES * elems
    left_q = (QUANT + 1) // 2
    depth = up(3 * basis, 16)
    turn_depth = up(3 * node_pad, 16)
    item_row = 4 * node_pad
    pair = 2 * node_pad
    first_q = (0, 3, 6)
    rest_q = tuple(q for q in range(QUANT) if q not in first_q)

    def odd_place():
        return lax.axis_index("row") % 2 == 1, lax.axis_index("col") % 2 == 1

    def predict_kernel(ins, outs, moved_ref, piece_ref, table_ref, star_sem):
        kxi_at, part_at, item_at, fault_at, dofs_at, star_at, send_at = 0, 1, 2, 3, 7, 8, 9
        proj_at, orient_at, lift_at, near_at, code_at = range(10, 15)
        asked_at, slot_at, work_at, sends_at = 0, 1, 2, 3
        back_table_at, trace_table_at, turn_table_at, lift_table_at = range(7, 11)
        near_out, code_out, star_out = range(11, 14)
        star_move = pltpu.make_async_copy(ins.sources[star_at], outs[star_out], star_sem)
        star_move.start()
        kxi_ref = ins[kxi_at]
        table_ref[...] = table(jnp.concatenate([kxi_ref[d].T for d in range(DIMS)], axis=0))
        by_row = lax.broadcasted_iota(jnp.int32, (faults, faults), 0)
        by_lane = lax.broadcasted_iota(jnp.int32, (faults, faults), 1)
        across = ins[part_at][...]
        wide = jnp.broadcast_to(across, (faults, faults))
        down = jnp.sum(jnp.where(by_row == by_lane, wide, 0), axis=1, keepdims=True)
        rank = jnp.sum(
            jnp.where((down == across) & (by_row < by_lane), 1, 0), axis=0, keepdims=True
        )
        place = across * slot_most + rank
        outs[slot_at][...] = place
        outs.flush(slot_at)
        chosen = one_hot(0, slots, place)
        item = (ins[item_at][...] + 1).astype(f32)
        rows = [pad_rows(ins[fault_at + i][...], node_pad) for i in range(4)]
        rows.append(pad_rows(item, LANES - item_row))
        head, rest = split(jnp.concatenate(rows, axis=0))
        outs[asked_at][...] = lax.dot_general(
            jnp.concatenate([chosen, chosen], axis=1),
            jnp.concatenate([head, rest], axis=1).astype(half),
            (((1,), (1,)), ((), ())),
            preferred_element_type=f32,
        )
        outs.flush(asked_at)

        proj_ref, orient_ref, lift_ref = ins[proj_at], ins[orient_at], ins[lift_at]
        outs[back_table_at][...] = table(
            jnp.concatenate([kxi_ref[d] for d in range(DIMS)], axis=0)
        )
        outs[trace_table_at][...] = table(
            jnp.concatenate([pad_rows(proj_ref[:, j, :], node_pad) for j in range(FACES)], axis=0)
        )
        outs[turn_table_at][...] = table(
            jnp.concatenate(
                [pad_lanes(pad_rows(orient_ref[t].T, node_pad), node_pad) for t in range(TURNS)],
                axis=0,
            )
        )
        outs[lift_table_at][...] = jnp.concatenate(
            [table(pad_lanes(lift_ref[:, j, :].T, node_pad)) for j in range(FACES)], axis=1
        )
        outs.flush(lift_table_at)
        odd_row, odd_col = odd_place()
        near = flat_row(ins[near_at])
        block = (near // ghosts) % 4
        flip = jnp.where(block < 2, jnp.where(odd_row, 0, 1), jnp.where(odd_col, 0, 1))
        outs[near_out][...] = jnp.where(
            near < sides_all, near, near + ghosts * flip * (1 - 2 * (block % 2))
        )
        outs[code_out][...] = flat_row(ins[code_at])

        dofs_ref, work_ref = ins[dofs_at], outs[work_at]
        for q in range(QUANT):
            start = dofs_ref[q * basis : (q + 1) * basis, :]
            work_ref[q * basis : (q + 1) * basis, :] = time_step * start
            piece_ref[q] = pieces(start)
        star_ref = outs[star_out]
        star_move.wait()

        def advance(order_k, factor):
            for q in range(QUANT):
                moved_ref[q] = product(table_ref[...], piece_ref[q])
            factor = factor * time_step / (order_k + 1).astype(f32)
            for side in range(sides):
                lanes = slice(side * LANES, (side + 1) * LANES)

                def emit(p, value):
                    piece_ref[p, :, lanes] = pieces(value)
                    rows = slice(p * basis, (p + 1) * basis)
                    work_ref[rows, lanes] = work_ref[rows, lanes] + factor * value

                star_apply(star_ref, moved_ref, basis, side, emit)
            return factor

        lax.fori_loop(1, ORDER, advance, f32(time_step))
        outs.flush(work_at)
        picks = ins[send_at][...]
        picks = jnp.concatenate([picks, picks], axis=1)
        order = [
            jnp.where(odd_row, picks[1:2], picks[0:1]),
            jnp.where(odd_row, picks[0:1], picks[1:2]),
            jnp.where(odd_col, picks[3:4], picks[2:3]),
            jnp.where(odd_col, picks[2:3], picks[3:4]),
        ]
        width = 2 * ghosts
        chosen = jnp.concatenate([one_hot(0, elems, order[d]) for d in range(4)], axis=1)
        low = lax.broadcasted_iota(jnp.int32, (basis, width), 1) < ghosts
        got = []
        for q in range(QUANT):
            head, rest = split(work_ref[q * basis : (q + 1) * basis, :])
            both = product(jnp.concatenate([head, rest], axis=0).astype(half), chosen)
            got.append(both[:basis] + both[basis:])
        for d in range(4):
            lanes = slice(d * width, (d + 1) * width)
            for q in range(left_q):
                first = got[q][:, lanes]
                second = got[q + left_q][:, lanes] if q + left_q < QUANT else first
                outs[sends_at + d][q * basis : (q + 1) * basis, :] = jnp.where(low, first, second)

    def local_kernel(ins, outs, moved_ref, trace_ref, left_ref, chosen_ref):
        near_at, back_table_at, trace_table_at, work_at, star_at, flux_at = range(6)
        seen_at, fric_at, volume_at, own_at = range(4)
        back_table, trace_table = ins[back_table_at][...], ins[trace_table_at][...]
        work_ref = ins[work_at]
        for q in range(QUANT):
            right = pieces(work_ref[q * basis : (q + 1) * basis, :])
            moved_ref[q] = product(back_table, right)
            got = product(trace_table, right)
            trace_ref[q] = got
            for j in range(FACES):
                head, rest = split(got[j * node_pad : (j + 1) * node_pad])
                left_ref[q * pair : (q + 1) * pair, j * elems : (j + 1) * elems] = jnp.concatenate(
                    [head, rest], axis=0
                ).astype(half)
        star_ref, volume_ref = ins[star_at], outs[volume_at]
        for side in range(sides):
            lanes = slice(side * LANES, (side + 1) * LANES)

            def emit(p, value):
                volume_ref[p * basis : (p + 1) * basis, lanes] = value

            star_apply(star_ref, moved_ref, basis, side, emit)
        outs.flush(volume_at)
        flux_ref, own_ref = ins[flux_at], outs[own_at]
        for side in range(sides):
            lanes = slice(side * LANES, (side + 1) * LANES)
            for j in range(FACES):
                totals = flux_apply(
                    flux_ref,
                    0,
                    lambda q: trace_ref[q, j * node_pad : (j + 1) * node_pad, lanes],
                    j,
                    side,
                    [None] * QUANT,
                )
                for p in range(QUANT):
                    at = (j * QUANT + p) * node_pad
                    own_ref[at : at + node_pad, lanes] = totals[p]
        outs.flush(own_at)
        near = ins[near_at][...]
        for j in range(FACES):
            chosen_ref[j * elems : (j + 1) * elems, :] = one_hot(j * elems, elems, near)
        outs[seen_at][...] = product(left_ref[...], chosen_ref[...]).astype(half)
        fric_ref = outs[fric_at]
        for j in range(FACES):
            rows = slice(j * node_pad, (j + 1) * node_pad)
            lanes = slice(j * elems, (j + 1) * elems)
            fric_ref[:node_pad, lanes] = 0.5 * (trace_ref[3, rows] + trace_ref[6, rows])
            fric_ref[node_pad:, lanes] = 0.5 * trace_ref[0, rows]

    def seen_across(
        got_refs, quants, trace_table, turn_table, near, code, seen_ref, chosen_ref, left_ref, emit
    ):
        low = lax.broadcasted_iota(jnp.int32, (basis, 2 * ghosts), 1) < ghosts
        for j in range(FACES):
            chosen_ref[j * ghost_all : (j + 1) * ghost_all, :] = one_hot(
                sides_all + j * ghost_all, ghost_all, near
            )
        for at, q in enumerate(quants):
            halves = []
            for first, second in (got_refs[:2], got_refs[2:]):
                if q < left_q:
                    rows = slice(q * basis, (q + 1) * basis)
                    a, b = first[rows, :], pltpu.roll(second[rows, :], ghosts, 1)
                else:
                    rows = slice((q - left_q) * basis, (q - left_q + 1) * basis)
                    a, b = pltpu.roll(first[rows, :], ghosts, 1), second[rows, :]
                halves.append(jnp.where(low, a, b))
            got = product(trace_table, pieces(jnp.concatenate(halves, axis=1)))
            for j in range(FACES):
                head, rest = split(got[j * node_pad : (j + 1) * node_pad])
                left_ref[
                    at * pair : (at + 1) * pair, j * ghost_all : (j + 1) * ghost_all
                ] = jnp.concatenate([head, rest], axis=0).astype(half)
        found = product(left_ref[...], chosen_ref[...])
        is_zero = jnp.broadcast_to(code, (node_pad, sides_all)) == 0
        is_one = jnp.broadcast_to(code, (node_pad, sides_all)) == 1
        for at, q in enumerate(quants):
            both = found[at * pair : (at + 1) * pair]
            both = both + seen_ref[q * pair : (q + 1) * pair].astype(f32)
            right = pad_rows(jnp.concatenate([both, both[:node_pad]], axis=0), turn_depth)
            rotated = product(turn_table, right.astype(half))
            emit(
                q,
                jnp.where(
                    is_zero,
                    rotated[:node_pad],
                    jnp.where(is_one, rotated[node_pad : 2 * node_pad], rotated[2 * node_pad :]),
                ),
            )

    def friction_kernel(ins, outs, chosen_ref, left_ref):
        got_at = range(4)
        trace_table_at, turn_table_at, near_at, code_at, seen_at, fric_at, asked_at = range(4, 11)
        back_at, turned_at, slip_at = range(3)
        kept = {}

        def emit(q, value):
            kept[q] = value
            at = first_q.index(q)
            outs[turned_at][at * node_pad : (at + 1) * node_pad, :] = value

        seen_across(
            [ins[i] for i in got_at],
            first_q,
            ins[trace_table_at][...],
            ins[turn_table_at][...],
            ins[near_at][...],
            ins[code_at][...],
            ins[seen_at],
            chosen_ref,
            left_ref,
            emit,
        )
        outs.flush(turned_at)
        fric_ref = ins[fric_at]
        shear = fric_ref[:node_pad, :] + 0.5 * (kept[3] - kept[6])
        normal = fric_ref[node_pad:, :] + 0.5 * kept[0]
        asked = ins[asked_at][...].T
        item = asked[item_row : item_row + 1, :].astype(jnp.int32) - 1
        wanted = one_hot(0, sides_all, item)
        shear_head, shear_rest = split(shear)
        normal_head, normal_rest = split(normal)
        taken = product(
            jnp.concatenate([shear_head, shear_rest, normal_head, normal_rest], axis=0).astype(half),
            wanted,
        )
        own = [asked[i * node_pad : (i + 1) * node_pad] for i in range(4)]
        slip = friction_solve(
            taken[:node_pad] + taken[node_pad : 2 * node_pad],
            taken[2 * node_pad : 3 * node_pad] + taken[3 * node_pad :],
            *own,
        )
        outs[back_at][...] = pad_rows(slip, LANES).T
        outs[slip_at][...] = slip
        outs.flush(slip_at)

    def final_kernel(ins, outs, turned_ref, mixed_ref, chosen_ref, left_ref):
        got_at = range(4)
        trace_table_at, turn_table_at, near_at, code_at, seen_at, asked_at, slip_at = range(4, 11)
        first_at, flux_at, own_at, lift_table_at, volume_at, dofs_at = range(11, 17)

        def emit(q, value):
            turned_ref[q * node_pad : (q + 1) * node_pad, :] = value

        seen_across(
            [ins[i] for i in got_at],
            rest_q,
            ins[trace_table_at][...],
            ins[turn_table_at][...],
            ins[near_at][...],
            ins[code_at][...],
            ins[seen_at],
            chosen_ref,
            left_ref,
            emit,
        )
        for at, q in enumerate(first_q):
            emit(q, ins[first_at][at * node_pad : (at + 1) * node_pad, :])
        asked = ins[asked_at][...].T
        item = asked[item_row : item_row + 1, :].astype(jnp.int32) - 1
        wanted = one_hot(0, sides_all, item)
        slip_head, slip_rest = split(ins[slip_at][...])
        pushed = lax.dot_general(
            jnp.concatenate([slip_head, slip_rest], axis=0).astype(half),
            wanted,
            (((1,), (1,)), ((), ())),
            preferred_element_type=f32,
        )
        pushed = 2.0 * (pushed[:node_pad] + pushed[node_pad:])
        own_ref, flux_ref = ins[own_at], ins[flux_at]
        for side in range(sides):
            lanes = slice(side * LANES, (side + 1) * LANES)
            for j in range(FACES):
                at = j * elems + side * LANES
                rows_of = lambda p: slice((j * QUANT + p) * node_pad, (j * QUANT + p + 1) * node_pad)
                totals = [own_ref[rows_of(p), lanes] for p in range(QUANT)]
                push = pushed[:, at : at + LANES]
                totals[3] = totals[3] - push
                totals[6] = totals[6] + push
                totals = flux_apply(
                    flux_ref,
                    1,
                    lambda q: turned_ref[q * node_pad : (q + 1) * node_pad, at : at + LANES],
                    j,
                    side,
                    totals,
                )
                for p in range(QUANT):
                    mixed_ref[p, j * turn_depth : (j + 1) * turn_depth, lanes] = pieces(totals[p])
        lift_table, volume_ref, dofs_ref = ins[lift_table_at][...], ins[volume_at], ins[dofs_at]
        for p in range(QUANT):
            rows = slice(p * basis, (p + 1) * basis)
            lifted = volume_ref[rows, :] + product(lift_table, mixed_ref[p])
            outs[0][rows, :] = dofs_ref[rows, :] + 0.25 * lifted
            outs.flush(0, rows)

    def return_kernel(ins, outs):
        chosen = one_hot(0, slots, ins[0][...])
        head, rest = split(ins[1][...].T[:node_pad])
        got = product(jnp.concatenate([head, rest], axis=0).astype(half), chosen)
        outs[0][...] = (got[:node_pad] + got[node_pad:])[:nodes]

    vmem = pltpu.VMEM
    proj_rows = jnp.transpose(face_proj, (2, 0, 1))
    lift_rows = jnp.transpose(face_lift, (1, 0, 2))
    *first_outs, back_table, trace_table, turn_table, lift_table, near, code, star_kept = call(
        predict_kernel,
        "predict",
        [
            kxi,
            fault_part.reshape(1, faults),
            fault_item.reshape(1, faults),
            shear_init,
            normal_init,
            state_var,
            slip_prev,
            dofs,
            Left(star),
            send_list,
            proj_rows,
            orient,
            lift_rows,
            neighbour,
            orient_code,
        ],
        [
            ((slots, LANES), f32, "hbm"),
            ((1, faults), jnp.int32, "vmem"),
            (dofs.shape, f32, "vmem"),
        ]
        + [((left_q * basis, 2 * ghosts), f32, "any")] * 4
        + [
            ((DIMS * basis, depth), half, "vmem"),
            ((FACES * node_pad, depth), half, "vmem"),
            ((TURNS * node_pad, turn_depth), half, "vmem"),
            ((basis, FACES * turn_depth), half, "hbm"),
            ((1, sides_all), jnp.int32, "vmem"),
            ((1, sides_all), jnp.int32, "vmem"),
            (star.shape, f32, "vmem"),
        ],
        scratch=(
            vmem((QUANT, DIMS * basis, elems), f32),
            vmem((QUANT, depth, elems), half),
            vmem((DIMS * basis, depth), half),
            pltpu.SemaphoreType.DMA,
        ),
        flops=5 * 2 * DIMS * basis * depth * QUANT * elems,
        moved=8_000_000,
    )

    asked, slot_of, work, *sends = first_outs
    asked = lax.all_to_all(
        asked.reshape(devices, slot_most, LANES), ("row", "col"), split_axis=0, concat_axis=0, tiled=True
    ).reshape(slots, LANES)

    def swapped(values, axis, first):
        pairs = [(i, i + 1) for i in range(first, lax.axis_size(axis) - 1, 2)]
        return lax.ppermute(values, axis, pairs + [(b, a) for a, b in pairs])

    arrived = [
        swapped(sends[0], "row", 0),
        swapped(sends[1], "row", 1),
        swapped(sends[2], "col", 0),
        swapped(sends[3], "col", 1),
    ]

    seen, fric, volume, own = call(
        local_kernel,
        "local_terms",
        [*(Kept(one) for one in (near, back_table, trace_table, work, star_kept)), flux_mats],
        [
            ((QUANT * pair, sides_all), half, "vmem"),
            ((pair, sides_all), f32, "vmem"),
            (dofs.shape, f32, "hbm"),
            ((FACES * QUANT * node_pad, elems), f32, "hbm"),
        ],
        scratch=(
            vmem((QUANT, DIMS * basis, elems), f32),
            vmem((QUANT, FACES * node_pad, elems), f32),
            vmem((QUANT * pair, sides_all), half),
            vmem((sides_all, sides_all), half),
        ),
        flops=2 * QUANT * pair * sides_all * sides_all,
        moved=8_000_000,
    )

    back, first_turned, slip = call(
        friction_kernel,
        "friction",
        [Kept(one) for one in (*arrived, trace_table, turn_table, near, code, seen, fric, asked)],
        [
            ((slots, LANES), f32, "any"),
            ((len(first_q) * node_pad, sides_all), f32, "vmem"),
            ((node_pad, slots), f32, "vmem"),
        ],
        scratch=(vmem((FACES * ghost_all, sides_all), half), vmem((len(first_q) * pair, FACES * ghost_all), half),),
        flops=2 * len(first_q) * pair * sides_all * sides_all,
        moved=4_000_000,
    )
    back = lax.all_to_all(
        back.reshape(devices, slot_most, LANES), ("row", "col"), split_axis=0, concat_axis=0, tiled=True
    ).reshape(slots, LANES)

    (dofs_next,) = call(
        final_kernel,
        "final_terms",
        [
            *(Kept(one) for one in arrived),
            Kept(trace_table),
            Kept(turn_table),
            Kept(near),
            Kept(code),
            Kept(seen),
            Kept(asked),
            Kept(slip),
            Kept(first_turned),
            flux_mats,
            own,
            lift_table,
            volume,
            dofs,
        ],
        [(dofs.shape, f32, "hbm")],
        scratch=(
            vmem((QUANT * node_pad, sides_all), f32),
            vmem((QUANT, FACES * turn_depth, elems), half),
            vmem((FACES * ghost_all, sides_all), half),
            vmem((len(rest_q) * pair, FACES * ghost_all), half),
        ),
        flops=2 * QUANT * pair * sides_all * sides_all,
        moved=8_000_000,
        flushes=QUANT,
    )

    (slip_rate,) = call(
        return_kernel,
        "fault_return",
        [Kept(slot_of), Kept(back)],
        [((nodes, faults), f32, "any")],
        flops=2 * pair * slots * faults,
        moved=200_000,
    )
    return dofs_next, slip_rate


def solution(mesh):
    across = ("row", "col")
    placed = (
        P(None, across),
        P(None, across),
        P(None, across),
        P(),
        P(),
        P(),
        P(),
        P(None, across),
        P(None, across),
        P(None, across),
        P(across, None),
        P(across),
        P(None, across),
        P(None, across),
        P(None, across),
        P(None, across),
    )
    return jax.shard_map(
        per_device,
        mesh=mesh,
        in_specs=placed,
        out_specs=(P(None, across), P(None, across)),
        check_vma=False,
    )
```

time: 62.1 us -> 48.2 us (0.78)
  local copies, waits for them, and re-layouts: 9.49 us -> 0 us
  Pallas kernels: 20.4 us -> 25.9 us
  starting transfers between devices: 24.5 us -> 19.7 us
  waiting for transfers between devices: 6.01 us -> 1.48 us
    unnamed x47 -> x0, local copies, waits for them, and re-layouts: 9.49 us -> none
    ppermute x4, starting transfers between devices: 8.82 us -> 3.23 us  [swapped(): return lax.ppermute(values, axis, pairs + [(b, a) for a, b in pairs])]
    pallas_call x6 -> x5, Pallas kernels: 20.4 us -> 25.9 us  [call(): pl.pallas_call(body, name=name, out_shape=shapes, in_specs=[pl.BlockSpec(...]
    all_to_all x1, waiting for transfers between devices: 6 us -> 1.47 us  [per_device(): lax.all_to_all(back.reshape(devices, slot_most, LANES), ('row', 'col'), s...]
    all_to_all x1, starting transfers between devices: 8.43 us -> 9.16 us  [per_device(): lax.all_to_all(back.reshape(devices, slot_most, LANES), ('row', 'col'), s...]
where the time goes in v1:
time: 48.2 us; the launch traced here: 47.9 us
  Pallas kernels  25.9 us (54%)
  starting transfers between devices  19.7 us (41%)
  waiting for transfers between devices  1.48 us (3%)
  between operations  0.75 us (2%)
    pallas_call x5, Pallas kernels, call(): pl.pallas_call(body, name=name, out_shape=shapes, in_specs=[pl.BlockSpec(...  25.9 us
    all_to_all x1, starting transfers between devices, per_device(): lax.all_to_all(back.reshape(devices, slot_most, LANES), ('row', 'col'), s...  9.16 us
    all_to_all x1, starting transfers between devices, per_device(): lax.all_to_all(asked.reshape(devices, slot_most, LANES), ('row', 'col'),...  7.31 us
    ppermute x4, starting transfers between devices, swapped(): return lax.ppermute(values, axis, pairs + [(b, a) for a, b in pairs])  3.23 us
    all_to_all x1, waiting for transfers between devices, per_device(): lax.all_to_all(back.reshape(devices, slot_most, LANES), ('row', 'col'), s...  1.47 us
  transfers between devices with their start and end apart: 6, of which 1 were waited for; matrix products, arithmetic and copies ran while one was open for 0% of the time, Pallas kernels for 24%

profile of v1, /device:TPU:0, one launch (start us, length us, event | category | flops | bytes accessed | tf_op | source)
XLA Modules:
  0.0 47.9 jit_solution(6246051372586168327)
XLA Ops:
  0.6 11.4 %predict.1 = (f32[256,128]{1,0:T(8,128)}, s32[1,128]{1,0:T(1,128)S(1)}, f32[504,256]{1,0:T(8,128)S(1)}, f32[280,128]{1,0:T(8,128)S(1)}, f32[280,128]{1,0:T(8,128...) custom-call(f32[3,56,56]{2,1,0:T(8,128)} %refs_0_.1, ...), custom_call_target="tpu_custom_call" | custom-call | flops 681246720 | bytes 8000000 | tf_op jit(solution)/shard_map/predict/pallas_call | solution.py:211
  12.0 7.3 %all-to-all-start = ((f32[32,8,128]{2,1,0:T(8,128)}), f32[32,8,128]{2,1,0:T(8,128)S(1)}, u32[]{:S(2)}, u32[]{:S(2)}) async-start(f32[32,8,128]{2,1,0:T(8,128)} %bitcast.11), calls=%async_computation | async-start | bytes 262144 | tf_op jit(solution)/shard_map/all_to_all | solution.py:630
  19.3 1.8 %collective-permute-start = (f32[280,128]{1,0:T(8,128)S(1)}, f32[280,128]{1,0:T(8,128)S(1)}, u32[]{:S(2)}, u32[]{:S(2)}) collective-permute-start(f32[280,128]{1,0:T(8,128)S(1)} %get-tuple-element.23), channel_id=1, source_target_pairs={{0,8},{16,24},{8,0},{24,16},{1,9},{17,25},{9,1},{25,17},{2,10},{18... | collective-permute-start | bytes 430088 | tf_op jit(solution)/shard_map/ppermute | solution.py:636
  21.2 0.7 %collective-permute-start.1 = (f32[280,128]{1,0:T(8,128)S(1)}, f32[280,128]{1,0:T(8,128)S(1)}, u32[]{:S(2)}, u32[]{:S(2)}) collective-permute-start(f32[280,128]{1,0:T(8,128)S(1)} %get-tuple-element.24), channel_id=1, source_target_pairs={{8,16},{16,8},{9,17},{17,9},{10,18},{18,10},{11,19},{19,11},{12,20... | collective-permute-start | bytes 430088 | tf_op jit(solution)/shard_map/ppermute | solution.py:636
  21.8 0.1 collective-permute-start.2
  21.9 0.7 %collective-permute-start.3 = (f32[280,128]{1,0:T(8,128)S(1)}, f32[280,128]{1,0:T(8,128)S(1)}, u32[]{:S(2)}, u32[]{:S(2)}) collective-permute-start(f32[280,128]{1,0:T(8,128)S(1)} %get-tuple-element.26), channel_id=1, source_target_pairs={{1,2},{3,4},{5,6},{2,1},{4,3},{6,5},{9,10},{11,12},{13,14},{10,9},... | collective-permute-start | bytes 430088 | tf_op jit(solution)/shard_map/ppermute | solution.py:636
  22.6 4.9 %local_terms.1 = (bf16[432,1024]{1,0:T(8,128)(2,1)S(1)}, f32[48,1024]{1,0:T(8,128)S(1)}, f32[504,256]{1,0:T(8,128)}, f32[864,256]{1,0:T(8,128)}) custom-call(s32[1,1024]{1,0:T(1,128)S(1)} %get-tuple-element.29.refs_0_.refs_6_, bf16[168,176]{1,0:T(8,128)(2,1)S(1)} %get-tuple-element.31.refs_1_, bf16[96,176]{1,0:T(8,128)(2,1)S(1)} %get-tuple-element.27.refs_2_.refs_4_, ...), custom_call_target="tpu_custom_call" | custom-call | flops 905969664 | bytes 8000000 | tf_op jit(solution)/shard_map/local_terms/pallas_call | solution.py:211
  27.5 0.0 collective-permute-done.refs_0_
  27.5 0.0 collective-permute-done.1.refs_1_
  27.5 0.0 collective-permute-done.2.refs_2_
  27.5 0.0 collective-permute-done.3.refs_3_
  27.5 0.0 all-to-all-done
  27.5 2.1 %friction.1 = (f32[256,128]{1,0:T(8,128)}, f32[72,1024]{1,0:T(8,128)S(1)}, f32[24,256]{1,0:T(8,128)S(1)}) custom-call(f32[280,128]{1,0:T(8,128)S(1)} %collective-permute-done.refs_0_, f32[280,128]{1,0:T(8,128)S(1)} %collective-permute-done.1.refs_1_, f32[280,128]{1,0:T(8,128)S(1)} %collective-permute-done.2.refs_2_, ...), custom_call_target="tpu_custom_call" | custom-call | flops 301989888 | bytes 4000000 | tf_op jit(solution)/shard_map/friction/pallas_call | solution.py:211
  29.7 9.2 %all-to-all-start.1 = ((f32[32,8,128]{2,1,0:T(8,128)}), f32[32,8,128]{2,1,0:T(8,128)S(1)}, u32[]{:S(2)}, u32[]{:S(2)}) async-start(f32[32,8,128]{2,1,0:T(8,128)} %bitcast.6), calls=%async_computation.1 | async-start | bytes 262144 | tf_op jit(solution)/shard_map/all_to_all | solution.py:678
  38.9 6.7 %final_terms.1 = f32[504,256]{1,0:T(8,128)} custom-call(f32[280,128]{1,0:T(8,128)S(1)} %collective-permute-done.refs_0_, f32[280,128]{1,0:T(8,128)S(1)} %collective-permute-done.1.refs_1_, f32[280,128]{1,0:T(8,128)S(1)} %collective-permute-done.2.refs_2_, f32[280,128]{1,0:T(8,128)S(1)} %collective-permute-done.3.refs_3_, ...), custom_call_target="tpu_custom_call" | custom-call | flops 905969664 | bytes 8000000 | tf_op jit(solution)/shard_map/final_terms/pallas_call | solution.py:211
  45.6 1.5 %all-to-all-done.1 = f32[32,8,128]{2,1,0:T(8,128)S(1)} async-done(((f32[32,8,128]{2,1,0:T(8,128)}), f32[32,8,128]{2,1,0:T(8,128)S(1)}, u32[]{:S(2)}, u32[]{:S(2)}) %all-to-all-start.1) | async-done | bytes 131104 | tf_op jit(solution)/shard_map/all_to_all | solution.py:678
  47.0 0.8 %fault_return.1 = f32[21,128]{1,0:T(8,128)} custom-call(s32[1,128]{1,0:T(1,128)S(1)} %get-tuple-element.42.refs_0_, f32[256,128]{1,0:T(8,128)S(1)} %bitcast.10), custom_call_target="tpu_custom_call" | custom-call | flops 3145728 | bytes 200000 | tf_op jit(solution)/shard_map/fault_return/pallas_call | solution.py:211
Async XLA Ops:
  12.0 15.5 %all-to-all-start = ((f32[32,8,128]{2,1,0:T(8,128)}), f32[32,8,128]{2,1,0:T(8,128)S(1)}, u32[]{:S(2)}, u32[]{:S(2)}) async-start(f32[32,8,128]{2,1,0:T(8,128)} %bitcast.11), calls=%async_computation | async-start | bytes 262144 | tf_op jit(solution)/shard_map/all_to_all | solution.py:630
  19.3 8.2 %collective-permute-start = (f32[280,128]{1,0:T(8,128)S(1)}, f32[280,128]{1,0:T(8,128)S(1)}, u32[]{:S(2)}, u32[]{:S(2)}) collective-permute-start(f32[280,128]{1,0:T(8,128)S(1)} %get-tuple-element.23), channel_id=1, source_target_pairs={{0,8},{16,24},{8,0},{24,16},{1,9},{17,25},{9,1},{25,17},{2,10},{18... | collective-permute-start | bytes 430088 | tf_op jit(solution)/shard_map/ppermute | solution.py:636
  21.2 6.3 %collective-permute-start.1 = (f32[280,128]{1,0:T(8,128)S(1)}, f32[280,128]{1,0:T(8,128)S(1)}, u32[]{:S(2)}, u32[]{:S(2)}) collective-permute-start(f32[280,128]{1,0:T(8,128)S(1)} %get-tuple-element.24), channel_id=1, source_target_pairs={{8,16},{16,8},{9,17},{17,9},{10,18},{18,10},{11,19},{19,11},{12,20... | collective-permute-start | bytes 430088 | tf_op jit(solution)/shard_map/ppermute | solution.py:636
  21.8 5.7 %collective-permute-start.2 = (f32[280,128]{1,0:T(8,128)S(1)}, f32[280,128]{1,0:T(8,128)S(1)}, u32[]{:S(2)}, u32[]{:S(2)}) collective-permute-start(f32[280,128]{1,0:T(8,128)S(1)} %get-tuple-element.25), channel_id=1, source_target_pairs={{0,1},{2,3},{4,5},{6,7},{1,0},{3,2},{5,4},{7,6},{8,9},{10,11},{12,... | collective-permute-start | bytes 430088 | tf_op jit(solution)/shard_map/ppermute | solution.py:636
  21.9 5.6 %collective-permute-start.3 = (f32[280,128]{1,0:T(8,128)S(1)}, f32[280,128]{1,0:T(8,128)S(1)}, u32[]{:S(2)}, u32[]{:S(2)}) collective-permute-start(f32[280,128]{1,0:T(8,128)S(1)} %get-tuple-element.26), channel_id=1, source_target_pairs={{1,2},{3,4},{5,6},{2,1},{4,3},{6,5},{9,10},{11,12},{13,14},{10,9},... | collective-permute-start | bytes 430088 | tf_op jit(solution)/shard_map/ppermute | solution.py:636
  29.7 17.3 %all-to-all-start.1 = ((f32[32,8,128]{2,1,0:T(8,128)}), f32[32,8,128]{2,1,0:T(8,128)S(1)}, u32[]{:S(2)}, u32[]{:S(2)}) async-start(f32[32,8,128]{2,1,0:T(8,128)} %bitcast.6), calls=%async_computation.1 | async-start | bytes 262144 | tf_op jit(solution)/shard_map/all_to_all | solution.py:678

commit v2 on v1

--- a/solution.py
+++ b/solution.py
@@ -131,11 +131,6 @@
         self.array = array
 
 
-class Left:
-    def __init__(self, array):
-        self.array = array
-
-
 class Inputs:
     def __init__(self, sources, targets, sems):
         self.sources, self.targets, self.waiting = sources, targets, {}
@@ -182,8 +177,8 @@
     n_in, n_out = len(ins), len(outs)
     placed = [i for i, one in enumerate(outs) if one[2] == "hbm"]
     stays = [isinstance(one, Kept) for one in ins]
-    brought = [i for i in range(n_in) if not isinstance(ins[i], (Kept, Left))]
-    ins = [one.array if isinstance(one, (Kept, Left)) else one for one in ins]
+    brought = [i for i in range(n_in) if not isinstance(ins[i], Kept)]
+    ins = [one.array if isinstance(one, Kept) else one for one in ins]
     flushes = flushes or max(1, len(placed))
 
     def body(*refs):
@@ -261,19 +256,19 @@
     item_row = 4 * node_pad
     pair = 2 * node_pad
     first_q = (0, 3, 6)
-    rest_q = tuple(q for q in range(QUANT) if q not in first_q)
+    slot_lanes = up(node_pad, 32)
+    per_row = LANES // slot_lanes
+    chunk = slot_most * slot_lanes
+    chunk_shape = (chunk // LANES, LANES) if chunk % LANES == 0 else (chunk,)
 
     def odd_place():
         return lax.axis_index("row") % 2 == 1, lax.axis_index("col") % 2 == 1
 
-    def predict_kernel(ins, outs, moved_ref, piece_ref, table_ref, star_sem):
+    def predict_kernel(ins, outs, moved_ref, piece_ref, table_ref):
         kxi_at, part_at, item_at, fault_at, dofs_at, star_at, send_at = 0, 1, 2, 3, 7, 8, 9
-        proj_at, orient_at, lift_at, near_at, code_at = range(10, 15)
+        proj_at, orient_at, near_at, code_at = range(10, 14)
         asked_at, slot_at, work_at, sends_at = 0, 1, 2, 3
-        back_table_at, trace_table_at, turn_table_at, lift_table_at = range(7, 11)
-        near_out, code_out, star_out = range(11, 14)
-        star_move = pltpu.make_async_copy(ins.sources[star_at], outs[star_out], star_sem)
-        star_move.start()
+        trace_table_at, turn_table_at, near_out, code_out = range(7, 11)
         kxi_ref = ins[kxi_at]
         table_ref[...] = table(jnp.concatenate([kxi_ref[d].T for d in range(DIMS)], axis=0))
         by_row = lax.broadcasted_iota(jnp.int32, (faults, faults), 0)
@@ -300,10 +295,7 @@
         )
         outs.flush(asked_at)
 
-        proj_ref, orient_ref, lift_ref = ins[proj_at], ins[orient_at], ins[lift_at]
-        outs[back_table_at][...] = table(
-            jnp.concatenate([kxi_ref[d] for d in range(DIMS)], axis=0)
-        )
+        proj_ref, orient_ref = ins[proj_at], ins[orient_at]
         outs[trace_table_at][...] = table(
             jnp.concatenate([pad_rows(proj_ref[:, j, :], node_pad) for j in range(FACES)], axis=0)
         )
@@ -313,10 +305,6 @@
                 axis=0,
             )
         )
-        outs[lift_table_at][...] = jnp.concatenate(
-            [table(pad_lanes(lift_ref[:, j, :].T, node_pad)) for j in range(FACES)], axis=1
-        )
-        outs.flush(lift_table_at)
         odd_row, odd_col = odd_place()
         near = flat_row(ins[near_at])
         block = (near // ghosts) % 4
@@ -331,8 +319,7 @@
             start = dofs_ref[q * basis : (q + 1) * basis, :]
             work_ref[q * basis : (q + 1) * basis, :] = time_step * start
             piece_ref[q] = pieces(start)
-        star_ref = outs[star_out]
-        star_move.wait()
+        star_ref = ins[star_at]
 
         def advance(order_k, factor):
             for q in range(QUANT):
@@ -374,56 +361,48 @@
                 second = got[q + left_q][:, lanes] if q + left_q < QUANT else first
                 outs[sends_at + d][q * basis : (q + 1) * basis, :] = jnp.where(low, first, second)
 
-    def local_kernel(ins, outs, moved_ref, trace_ref, left_ref, chosen_ref):
-        near_at, back_table_at, trace_table_at, work_at, star_at, flux_at = range(6)
-        seen_at, fric_at, volume_at, own_at = range(4)
-        back_table, trace_table = ins[back_table_at][...], ins[trace_table_at][...]
+    def asked_item(asked):
+        return asked[item_row : item_row + 1, :].astype(jnp.int32) - 1
+
+    def local_kernel(ins, outs, left_ref, chosen_ref, wanted_ref):
+        near_at, trace_table_at, work_at, code_at, asked_at = range(5)
+        seen_at, fric_at, slot_seen_at, slot_near_at, slot_code_at = range(5)
+        trace_table = ins[trace_table_at][...]
         work_ref = ins[work_at]
+        kept = {}
         for q in range(QUANT):
-            right = pieces(work_ref[q * basis : (q + 1) * basis, :])
-            moved_ref[q] = product(back_table, right)
-            got = product(trace_table, right)
-            trace_ref[q] = got
+            got = product(trace_table, pieces(work_ref[q * basis : (q + 1) * basis, :]))
+            if q in first_q:
+                kept[q] = got
             for j in range(FACES):
                 head, rest = split(got[j * node_pad : (j + 1) * node_pad])
                 left_ref[q * pair : (q + 1) * pair, j * elems : (j + 1) * elems] = jnp.concatenate(
                     [head, rest], axis=0
                 ).astype(half)
-        star_ref, volume_ref = ins[star_at], outs[volume_at]
-        for side in range(sides):
-            lanes = slice(side * LANES, (side + 1) * LANES)
-
-            def emit(p, value):
-                volume_ref[p * basis : (p + 1) * basis, lanes] = value
-
-            star_apply(star_ref, moved_ref, basis, side, emit)
-        outs.flush(volume_at)
-        flux_ref, own_ref = ins[flux_at], outs[own_at]
-        for side in range(sides):
-            lanes = slice(side * LANES, (side + 1) * LANES)
-            for j in range(FACES):
-                totals = flux_apply(
-                    flux_ref,
-                    0,
-                    lambda q: trace_ref[q, j * node_pad : (j + 1) * node_pad, lanes],
-                    j,
-                    side,
-                    [None] * QUANT,
-                )
-                for p in range(QUANT):
-                    at = (j * QUANT + p) * node_pad
-                    own_ref[at : at + node_pad, lanes] = totals[p]
-        outs.flush(own_at)
         near = ins[near_at][...]
         for j in range(FACES):
             chosen_ref[j * elems : (j + 1) * elems, :] = one_hot(j * elems, elems, near)
         outs[seen_at][...] = product(left_ref[...], chosen_ref[...]).astype(half)
-        fric_ref = outs[fric_at]
+        item = asked_item(ins[asked_at][...].T)
+        wanted_ref[...] = one_hot(0, sides_all, item)
+        near_head, near_rest = split(near.astype(f32))
+        shear, normal = [], []
         for j in range(FACES):
             rows = slice(j * node_pad, (j + 1) * node_pad)
-            lanes = slice(j * elems, (j + 1) * elems)
-            fric_ref[:node_pad, lanes] = 0.5 * (trace_ref[3, rows] + trace_ref[6, rows])
-            fric_ref[node_pad:, lanes] = 0.5 * trace_ref[0, rows]
+            shear.append(0.5 * (kept[3][rows] + kept[6][rows]))
+            normal.append(0.5 * kept[0][rows])
+        rows = [*split(jnp.concatenate(shear, axis=1)), *split(jnp.concatenate(normal, axis=1))]
+        rows += [near_head, near_rest, ins[code_at][...].astype(f32)]
+        rows = jnp.concatenate(rows, axis=0)
+        taken = product(pad_rows(rows, up(rows.shape[0], 16)).astype(half), wanted_ref[...])
+        outs[fric_at][:node_pad, :] = taken[:node_pad] + taken[node_pad:pair]
+        outs[fric_at][node_pad:, :] = taken[pair : pair + node_pad] + taken[pair + node_pad : 2 * pair]
+        slot_near = (taken[2 * pair : 2 * pair + 1] + taken[2 * pair + 1 : 2 * pair + 2]).astype(jnp.int32)
+        slot_near = jnp.where(item < 0, -1, slot_near)
+        outs[slot_near_at][...] = slot_near
+        outs[slot_code_at][...] = taken[2 * pair + 2 : 2 * pair + 3].astype(jnp.int32)
+        left = jnp.concatenate([left_ref[q * pair : (q + 1) * pair, :] for q in first_q], axis=0)
+        outs[slot_seen_at][...] = product(left, one_hot(0, sides_all, slot_near)).astype(half)
 
     def seen_across(
         got_refs, quants, trace_table, turn_table, near, code, seen_ref, chosen_ref, left_ref, emit
@@ -450,11 +429,11 @@
                     at * pair : (at + 1) * pair, j * ghost_all : (j + 1) * ghost_all
                 ] = jnp.concatenate([head, rest], axis=0).astype(half)
         found = product(left_ref[...], chosen_ref[...])
-        is_zero = jnp.broadcast_to(code, (node_pad, sides_all)) == 0
-        is_one = jnp.broadcast_to(code, (node_pad, sides_all)) == 1
+        is_zero = jnp.broadcast_to(code, (node_pad, code.shape[1])) == 0
+        is_one = jnp.broadcast_to(code, (node_pad, code.shape[1])) == 1
         for at, q in enumerate(quants):
             both = found[at * pair : (at + 1) * pair]
-            both = both + seen_ref[q * pair : (q + 1) * pair].astype(f32)
+            both = both + seen_ref[at * pair : (at + 1) * pair].astype(f32)
             right = pad_rows(jnp.concatenate([both, both[:node_pad]], axis=0), turn_depth)
             rotated = product(turn_table, right.astype(half))
             emit(
@@ -466,16 +445,14 @@
                 ),
             )
 
-    def friction_kernel(ins, outs, chosen_ref, left_ref):
+    def friction_kernel(ins, outs, chosen_ref, left_ref, wide_ref):
         got_at = range(4)
         trace_table_at, turn_table_at, near_at, code_at, seen_at, fric_at, asked_at = range(4, 11)
-        back_at, turned_at, slip_at = range(3)
+        back_at, slip_at = range(2)
         kept = {}
 
         def emit(q, value):
             kept[q] = value
-            at = first_q.index(q)
-            outs[turned_at][at * node_pad : (at + 1) * node_pad, :] = value
 
         seen_across(
             [ins[i] for i in got_at],
@@ -489,40 +466,34 @@
             left_ref,
             emit,
         )
-        outs.flush(turned_at)
         fric_ref = ins[fric_at]
-        shear = fric_ref[:node_pad, :] + 0.5 * (kept[3] - kept[6])
-        normal = fric_ref[node_pad:, :] + 0.5 * kept[0]
         asked = ins[asked_at][...].T
-        item = asked[item_row : item_row + 1, :].astype(jnp.int32) - 1
-        wanted = one_hot(0, sides_all, item)
-        shear_head, shear_rest = split(shear)
-        normal_head, normal_rest = split(normal)
-        taken = product(
-            jnp.concatenate([shear_head, shear_rest, normal_head, normal_rest], axis=0).astype(half),
-            wanted,
-        )
         own = [asked[i * node_pad : (i + 1) * node_pad] for i in range(4)]
         slip = friction_solve(
-            taken[:node_pad] + taken[node_pad : 2 * node_pad],
-            taken[2 * node_pad : 3 * node_pad] + taken[3 * node_pad :],
+            fric_ref[:node_pad, :] + 0.5 * (kept[3] - kept[6]),
+            fric_ref[node_pad:, :] + 0.5 * kept[0],
             *own,
         )
-        outs[back_at][...] = pad_rows(slip, LANES).T
+        wide_ref[...] = pad_rows(slip, LANES).T
+        packed = wide_ref[pl.ds(0, slots // per_row, stride=per_row), :]
+        for k in range(1, per_row):
+            part = wide_ref[pl.ds(k, slots // per_row, stride=per_row), :]
+            packed = packed + pltpu.roll(part, k * slot_lanes, 1)
+        outs[back_at][...] = packed
         outs[slip_at][...] = slip
         outs.flush(slip_at)
 
-    def final_kernel(ins, outs, turned_ref, mixed_ref, chosen_ref, left_ref):
+    def final_kernel(ins, outs, moved_ref, trace_ref, turned_ref, mixed_ref, chosen_ref, left_ref):
         got_at = range(4)
         trace_table_at, turn_table_at, near_at, code_at, seen_at, asked_at, slip_at = range(4, 11)
-        first_at, flux_at, own_at, lift_table_at, volume_at, dofs_at = range(11, 17)
+        work_at, lift_at, kxi_at, flux_at, star_at, dofs_at = range(11, 17)
 
         def emit(q, value):
             turned_ref[q * node_pad : (q + 1) * node_pad, :] = value
 
         seen_across(
             [ins[i] for i in got_at],
-            rest_q,
+            range(QUANT),
             ins[trace_table_at][...],
             ins[turn_table_at][...],
             ins[near_at][...],
@@ -532,11 +503,8 @@
             left_ref,
             emit,
         )
-        for at, q in enumerate(first_q):
-            emit(q, ins[first_at][at * node_pad : (at + 1) * node_pad, :])
         asked = ins[asked_at][...].T
-        item = asked[item_row : item_row + 1, :].astype(jnp.int32) - 1
-        wanted = one_hot(0, sides_all, item)
+        wanted = one_hot(0, sides_all, asked_item(asked))
         slip_head, slip_rest = split(ins[slip_at][...])
         pushed = lax.dot_general(
             jnp.concatenate([slip_head, slip_rest], axis=0).astype(half),
@@ -545,16 +513,29 @@
             preferred_element_type=f32,
         )
         pushed = 2.0 * (pushed[:node_pad] + pushed[node_pad:])
-        own_ref, flux_ref = ins[own_at], ins[flux_at]
+        kxi_ref, lift_ref, work_ref = ins[kxi_at], ins[lift_at], ins[work_at]
+        back_table = table(jnp.concatenate([kxi_ref[d] for d in range(DIMS)], axis=0))
+        lift_table = jnp.concatenate(
+            [table(pad_lanes(lift_ref[:, j, :].T, node_pad)) for j in range(FACES)], axis=1
+        )
+        trace_table = ins[trace_table_at][...]
+        for q in range(QUANT):
+            right = pieces(work_ref[q * basis : (q + 1) * basis, :])
+            moved_ref[q] = product(back_table, right)
+            trace_ref[q] = product(trace_table, right)
+        flux_ref = ins[flux_at]
         for side in range(sides):
             lanes = slice(side * LANES, (side + 1) * LANES)
             for j in range(FACES):
                 at = j * elems + side * LANES
-                rows_of = lambda p: slice((j * QUANT + p) * node_pad, (j * QUANT + p + 1) * node_pad)
-                totals = [own_ref[rows_of(p), lanes] for p in range(QUANT)]
-                push = pushed[:, at : at + LANES]
-                totals[3] = totals[3] - push
-                totals[6] = totals[6] + push
+                totals = flux_apply(
+                    flux_ref,
+                    0,
+                    lambda q: trace_ref[q, j * node_pad : (j + 1) * node_pad, lanes],
+                    j,
+                    side,
+                    [None] * QUANT,
+                )
                 totals = flux_apply(
                     flux_ref,
                     1,
@@ -563,25 +544,40 @@
                     side,
                     totals,
                 )
+                push = pushed[:, at : at + LANES]
+                totals[3] = totals[3] - push
+                totals[6] = totals[6] + push
                 for p in range(QUANT):
                     mixed_ref[p, j * turn_depth : (j + 1) * turn_depth, lanes] = pieces(totals[p])
-        lift_table, volume_ref, dofs_ref = ins[lift_table_at][...], ins[volume_at], ins[dofs_at]
+        star_ref, dofs_ref = ins[star_at], ins[dofs_at]
+        out_ref = outs[0]
+        for side in range(sides):
+            lanes = slice(side * LANES, (side + 1) * LANES)
+
+            def emit(p, value):
+                rows = slice(p * basis, (p + 1) * basis)
+                out_ref[rows, lanes] = dofs_ref[rows, lanes] + 0.25 * value
+
+            star_apply(star_ref, moved_ref, basis, side, emit)
         for p in range(QUANT):
             rows = slice(p * basis, (p + 1) * basis)
-            lifted = volume_ref[rows, :] + product(lift_table, mixed_ref[p])
-            outs[0][rows, :] = dofs_ref[rows, :] + 0.25 * lifted
-            outs.flush(0, rows)
+            out_ref[rows, :] = out_ref[rows, :] + 0.25 * product(lift_table, mixed_ref[p])
 
     def return_kernel(ins, outs):
-        chosen = one_hot(0, slots, ins[0][...])
-        head, rest = split(ins[1][...].T[:node_pad])
-        got = product(jnp.concatenate([head, rest], axis=0).astype(half), chosen)
+        place = ins[0][...]
+        held = ins[1][...].T
+        rows = slots // per_row
+        got = jnp.zeros((pair, faults), f32)
+        for k in range(per_row):
+            head, rest = split(held[k * slot_lanes : k * slot_lanes + node_pad])
+            chosen = one_hot(0, rows, jnp.where(place % per_row == k, place // per_row, -1))
+            got = got + product(jnp.concatenate([head, rest], axis=0).astype(half), chosen)
         outs[0][...] = (got[:node_pad] + got[node_pad:])[:nodes]
 
     vmem = pltpu.VMEM
     proj_rows = jnp.transpose(face_proj, (2, 0, 1))
     lift_rows = jnp.transpose(face_lift, (1, 0, 2))
-    *first_outs, back_table, trace_table, turn_table, lift_table, near, code, star_kept = call(
+    *first_outs, trace_table, turn_table, near, code = call(
         predict_kernel,
         "predict",
         [
@@ -593,11 +589,10 @@
             state_var,
             slip_prev,
             dofs,
-            Left(star),
+            star,
             send_list,
             proj_rows,
             orient,
-            lift_rows,
             neighbour,
             orient_code,
         ],
@@ -608,19 +603,15 @@
         ]
         + [((left_q * basis, 2 * ghosts), f32, "any")] * 4
         + [
-            ((DIMS * basis, depth), half, "vmem"),
             ((FACES * node_pad, depth), half, "vmem"),
             ((TURNS * node_pad, turn_depth), half, "vmem"),
-            ((basis, FACES * turn_depth), half, "hbm"),
             ((1, sides_all), jnp.int32, "vmem"),
             ((1, sides_all), jnp.int32, "vmem"),
-            (star.shape, f32, "vmem"),
         ],
         scratch=(
             vmem((QUANT, DIMS * basis, elems), f32),
             vmem((QUANT, depth, elems), half),
             vmem((DIMS * basis, depth), half),
-            pltpu.SemaphoreType.DMA,
         ),
         flops=5 * 2 * DIMS * basis * depth * QUANT * elems,
         moved=8_000_000,
@@ -642,42 +633,45 @@
         swapped(sends[3], "col", 1),
     ]
 
-    seen, fric, volume, own = call(
+    seen, fric, slot_seen, slot_near, slot_code = call(
         local_kernel,
         "local_terms",
-        [*(Kept(one) for one in (near, back_table, trace_table, work, star_kept)), flux_mats],
+        [Kept(one) for one in (near, trace_table, work, code, asked)],
         [
             ((QUANT * pair, sides_all), half, "vmem"),
-            ((pair, sides_all), f32, "vmem"),
-            (dofs.shape, f32, "hbm"),
-            ((FACES * QUANT * node_pad, elems), f32, "hbm"),
+            ((pair, slots), f32, "vmem"),
+            ((len(first_q) * pair, slots), half, "vmem"),
+            ((1, slots), jnp.int32, "vmem"),
+            ((1, slots), jnp.int32, "vmem"),
         ],
         scratch=(
-            vmem((QUANT, DIMS * basis, elems), f32),
-            vmem((QUANT, FACES * node_pad, elems), f32),
             vmem((QUANT * pair, sides_all), half),
             vmem((sides_all, sides_all), half),
+            vmem((sides_all, slots), half),
         ),
         flops=2 * QUANT * pair * sides_all * sides_all,
         moved=8_000_000,
     )
 
-    back, first_turned, slip = call(
+    back, slip = call(
         friction_kernel,
         "friction",
-        [Kept(one) for one in (*arrived, trace_table, turn_table, near, code, seen, fric, asked)],
         [
-            ((slots, LANES), f32, "any"),
-            ((len(first_q) * node_pad, sides_all), f32, "vmem"),
-            ((node_pad, slots), f32, "vmem"),
+            Kept(one)
+            for one in (*arrived, trace_table, turn_table, slot_near, slot_code, slot_seen, fric, asked)
         ],
-        scratch=(vmem((FACES * ghost_all, sides_all), half), vmem((len(first_q) * pair, FACES * ghost_all), half),),
-        flops=2 * len(first_q) * pair * sides_all * sides_all,
+        [((slots // per_row, LANES), f32, "any"), ((node_pad, slots), f32, "vmem")],
+        scratch=(
+            vmem((FACES * ghost_all, slots), half),
+            vmem((len(first_q) * pair, FACES * ghost_all), half),
+            vmem((slots, LANES), f32),
+        ),
+        flops=2 * len(first_q) * pair * sides_all * slots,
         moved=4_000_000,
     )
     back = lax.all_to_all(
-        back.reshape(devices, slot_most, LANES), ("row", "col"), split_axis=0, concat_axis=0, tiled=True
-    ).reshape(slots, LANES)
+        back.reshape(devices, *chunk_shape), ("row", "col"), split_axis=0, concat_axis=0, tiled=True
+    ).reshape(slots // per_row, LANES)
 
     (dofs_next,) = call(
         final_kernel,
@@ -691,23 +685,24 @@
             Kept(seen),
             Kept(asked),
             Kept(slip),
-            Kept(first_turned),
+            Kept(work),
+            lift_rows,
+            kxi,
             flux_mats,
-            own,
-            lift_table,
-            volume,
+            star,
             dofs,
         ],
-        [(dofs.shape, f32, "hbm")],
+        [(dofs.shape, f32, "any")],
         scratch=(
+            vmem((QUANT, DIMS * basis, elems), f32),
+            vmem((QUANT, FACES * node_pad, elems), f32),
             vmem((QUANT * node_pad, sides_all), f32),
             vmem((QUANT, FACES * turn_depth, elems), half),
             vmem((FACES * ghost_all, sides_all), half),
-            vmem((len(rest_q) * pair, FACES * ghost_all), half),
+            vmem((QUANT * pair, FACES * ghost_all), half),
         ),
         flops=2 * QUANT * pair * sides_all * sides_all,
         moved=8_000_000,
-        flushes=QUANT,
     )
 
     (slip_rate,) = call(

time: 48.2 us -> 45.6 us (0.946)
  waiting for transfers between devices: 1.48 us -> 5.49 us
  Pallas kernels: 25.9 us -> 22.2 us
  starting transfers between devices: 19.7 us -> 16.9 us
    all_to_all x1, waiting for transfers between devices: 0.01 us -> 4.92 us  [per_device(): lax.all_to_all(asked.reshape(devices, slot_most, LANES), ('row', 'col'),...]
    pallas_call x5, Pallas kernels: 25.9 us -> 22.2 us  [call(): pl.pallas_call(body, name=name, out_shape=shapes, in_specs=[pl.BlockSpec(...]
    all_to_all x1, starting transfers between devices: 9.16 us -> 6.36 us  [per_device(): lax.all_to_all(back.reshape(devices, *chunk_shape), ('row', 'col'), split...]
    all_to_all x1, waiting for transfers between devices: 1.47 us -> 0.56 us  [per_device(): lax.all_to_all(back.reshape(devices, *chunk_shape), ('row', 'col'), split...]
  transfers between devices with their start and end apart: 6 -> 6, of which waited for: 1 -> 2; matrix products, arithmetic and copies ran while one was open for 0% -> 0% of each run, Pallas kernels for 24% -> 19%
where the time goes in v2:
time: 45.6 us; the launch traced here: 45.3 us
  Pallas kernels  22.2 us (49%)
  starting transfers between devices  16.9 us (37%)
  waiting for transfers between devices  5.49 us (12%)
  between operations  0.74 us (2%)
    pallas_call x5, Pallas kernels, call(): pl.pallas_call(body, name=name, out_shape=shapes, in_specs=[pl.BlockSpec(...  22.2 us
    all_to_all x1, starting transfers between devices, per_device(): lax.all_to_all(asked.reshape(devices, slot_most, LANES), ('row', 'col'),...  7.3 us
    all_to_all x1, starting transfers between devices, per_device(): lax.all_to_all(back.reshape(devices, *chunk_shape), ('row', 'col'), split...  6.36 us
    all_to_all x1, waiting for transfers between devices, per_device(): lax.all_to_all(asked.reshape(devices, slot_most, LANES), ('row', 'col'),...  4.92 us
    ppermute x4, starting transfers between devices, swapped(): return lax.ppermute(values, axis, pairs + [(b, a) for a, b in pairs])  3.23 us
  transfers between devices with their start and end apart: 6, of which 2 were waited for; matrix products, arithmetic and copies ran while one was open for 0% of the time, Pallas kernels for 19%

profile of v2, /device:TPU:0, one launch (start us, length us, event | category | flops | bytes accessed | tf_op | source)
XLA Modules:
  0.0 45.3 jit_solution(10885651059384818902)
XLA Ops:
  0.6 11.3 %predict.1 = (f32[256,128]{1,0:T(8,128)}, s32[1,128]{1,0:T(1,128)S(1)}, f32[504,256]{1,0:T(8,128)S(1)}, f32[280,128]{1,0:T(8,128)S(1)}, f32[280,128]{1,0:T(8,128...) custom-call(f32[3,56,56]{2,1,0:T(8,128)} %refs_13_.3, ...), custom_call_target="tpu_custom_call" | custom-call | flops 681246720 | bytes 8000000 | tf_op jit(solution)/shard_map/predict/pallas_call | solution.py:206
  11.9 7.3 %all-to-all-start = ((f32[32,8,128]{2,1,0:T(8,128)}), f32[32,8,128]{2,1,0:T(8,128)S(1)}, u32[]{:S(2)}, u32[]{:S(2)}) async-start(f32[32,8,128]{2,1,0:T(8,128)} %bitcast.12), calls=%async_computation | async-start | bytes 262144 | tf_op jit(solution)/shard_map/all_to_all | solution.py:621
  19.2 1.8 %collective-permute-start = (f32[280,128]{1,0:T(8,128)S(1)}, f32[280,128]{1,0:T(8,128)S(1)}, u32[]{:S(2)}, u32[]{:S(2)}) collective-permute-start(f32[280,128]{1,0:T(8,128)S(1)} %get-tuple-element.20), channel_id=1, source_target_pairs={{0,8},{16,24},{8,0},{24,16},{1,9},{17,25},{9,1},{25,17},{2,10},{18... | collective-permute-start | bytes 430088 | tf_op jit(solution)/shard_map/ppermute | solution.py:627
  21.0 0.7 %collective-permute-start.1 = (f32[280,128]{1,0:T(8,128)S(1)}, f32[280,128]{1,0:T(8,128)S(1)}, u32[]{:S(2)}, u32[]{:S(2)}) collective-permute-start(f32[280,128]{1,0:T(8,128)S(1)} %get-tuple-element.21), channel_id=1, source_target_pairs={{8,16},{16,8},{9,17},{17,9},{10,18},{18,10},{11,19},{19,11},{12,20... | collective-permute-start | bytes 430088 | tf_op jit(solution)/shard_map/ppermute | solution.py:627
  21.7 0.1 collective-permute-start.2
  21.8 0.7 %collective-permute-start.3 = (f32[280,128]{1,0:T(8,128)S(1)}, f32[280,128]{1,0:T(8,128)S(1)}, u32[]{:S(2)}, u32[]{:S(2)}) collective-permute-start(f32[280,128]{1,0:T(8,128)S(1)} %get-tuple-element.23), channel_id=1, source_target_pairs={{1,2},{3,4},{5,6},{2,1},{4,3},{6,5},{9,10},{11,12},{13,14},{10,9},... | collective-permute-start | bytes 430088 | tf_op jit(solution)/shard_map/ppermute | solution.py:627
  22.5 4.9 %all-to-all-done = f32[32,8,128]{2,1,0:T(8,128)S(1)} async-done(((f32[32,8,128]{2,1,0:T(8,128)}), f32[32,8,128]{2,1,0:T(8,128)S(1)}, u32[]{:S(2)}, u32[]{:S(2)}) %all-to-all-start) | async-done | bytes 131104 | tf_op jit(solution)/shard_map/all_to_all | solution.py:621
  27.4 1.7 %local_terms.1 = (bf16[432,1024]{1,0:T(8,128)(2,1)S(1)}, f32[48,256]{1,0:T(8,128)S(1)}, bf16[144,256]{1,0:T(8,128)(2,1)S(1)}, s32[1,256]{1,0:T(1,128)S(1)}, s32[1,256]{1,0:T(1,128)S(1)}) custom-call(s32[1,1024]{1,0:T(1,128)S(1)} %get-tuple-element.26.refs_0_.refs_6_, bf16[96,176]{1,0:T(8,128)(2,1)S(1)} %get-tuple-element.24.refs_1_.refs_4_, ...), custom_call_target="tpu_custom_call" | custom-call | flops 905969664 | bytes 8000000 | tf_op jit(solution)/shard_map/local_terms/pallas_call | solution.py:206
  29.1 0.0 collective-permute-done.refs_0_
  29.1 0.0 collective-permute-done.1.refs_1_
  29.2 0.0 collective-permute-done.2.refs_2_
  29.2 0.0 collective-permute-done.3.refs_3_
  29.2 1.6 %friction.1 = (f32[64,128]{1,0:T(8,128)}, f32[24,256]{1,0:T(8,128)S(1)}) custom-call(f32[280,128]{1,0:T(8,128)S(1)} %collective-permute-done.refs_0_, f32[280,128]{1,0:T(8,128)S(1)} %collective-permute-done.1.refs_1_, f32[280,128]{1,0:T(8,128)S(1)} %collective-permute-done.2.refs_2_, f32[280,128]{1,0:T(8,128)S(1)} %collective-permute-done.3.refs_3_, ...), custom_call_target="tpu_custom_call" | custom-call | flops 75497472 | bytes 4000000 | tf_op jit(solution)/shard_map/friction/pallas_call | solution.py:206
  30.8 6.4 %all-to-all-start.1 = ((f32[32,2,128]{2,1,0:T(2,128)}), f32[32,2,128]{2,1,0:T(2,128)S(1)}, u32[]{:S(2)}, u32[]{:S(2)}) async-start(f32[32,2,128]{2,1,0:T(2,128)} %bitcast.6), calls=%async_computation.1 | async-start | bytes 65536 | tf_op jit(solution)/shard_map/all_to_all | solution.py:672
  37.2 6.7 %final_terms.1 = f32[504,256]{1,0:T(8,128)} custom-call(f32[280,128]{1,0:T(8,128)S(1)} %collective-permute-done.refs_0_, f32[280,128]{1,0:T(8,128)S(1)} %collective-permute-done.1.refs_1_, f32[280,128]{1,0:T(8,128)S(1)} %collective-permute-done.2.refs_2_, f32[280,128]{1,0:T(8,128)S(1)} %collective-permute-done.3.refs_3_, ...), custom_call_target="tpu_custom_call" | custom-call | flops 905969664 | bytes 8000000 | tf_op jit(solution)/shard_map/final_terms/pallas_call | solution.py:206
  43.9 0.6 %all-to-all-done.1 = f32[32,2,128]{2,1,0:T(2,128)S(1)} async-done(((f32[32,2,128]{2,1,0:T(2,128)}), f32[32,2,128]{2,1,0:T(2,128)S(1)}, u32[]{:S(2)}, u32[]{:S(2)}) %all-to-all-start.1) | async-done | bytes 32800 | tf_op jit(solution)/shard_map/all_to_all | solution.py:672
  44.4 0.9 %fault_return.1 = f32[21,128]{1,0:T(8,128)} custom-call(s32[1,128]{1,0:T(1,128)S(1)} %get-tuple-element.36.refs_0_, f32[64,128]{1,0:T(8,128)S(1)} %bitcast.11), custom_call_target="tpu_custom_call" | custom-call | flops 3145728 | bytes 200000 | tf_op jit(solution)/shard_map/fault_return/pallas_call | solution.py:206
Async XLA Ops:
  11.9 15.5 %all-to-all-start = ((f32[32,8,128]{2,1,0:T(8,128)}), f32[32,8,128]{2,1,0:T(8,128)S(1)}, u32[]{:S(2)}, u32[]{:S(2)}) async-start(f32[32,8,128]{2,1,0:T(8,128)} %bitcast.12), calls=%async_computation | async-start | bytes 262144 | tf_op jit(solution)/shard_map/all_to_all | solution.py:621
  19.2 9.9 %collective-permute-start = (f32[280,128]{1,0:T(8,128)S(1)}, f32[280,128]{1,0:T(8,128)S(1)}, u32[]{:S(2)}, u32[]{:S(2)}) collective-permute-start(f32[280,128]{1,0:T(8,128)S(1)} %get-tuple-element.20), channel_id=1, source_target_pairs={{0,8},{16,24},{8,0},{24,16},{1,9},{17,25},{9,1},{25,17},{2,10},{18... | collective-permute-start | bytes 430088 | tf_op jit(solution)/shard_map/ppermute | solution.py:627
  21.0 8.1 %collective-permute-start.1 = (f32[280,128]{1,0:T(8,128)S(1)}, f32[280,128]{1,0:T(8,128)S(1)}, u32[]{:S(2)}, u32[]{:S(2)}) collective-permute-start(f32[280,128]{1,0:T(8,128)S(1)} %get-tuple-element.21), channel_id=1, source_target_pairs={{8,16},{16,8},{9,17},{17,9},{10,18},{18,10},{11,19},{19,11},{12,20... | collective-permute-start | bytes 430088 | tf_op jit(solution)/shard_map/ppermute | solution.py:627
  21.7 7.5 %collective-permute-start.2 = (f32[280,128]{1,0:T(8,128)S(1)}, f32[280,128]{1,0:T(8,128)S(1)}, u32[]{:S(2)}, u32[]{:S(2)}) collective-permute-start(f32[280,128]{1,0:T(8,128)S(1)} %get-tuple-element.22), channel_id=1, source_target_pairs={{0,1},{2,3},{4,5},{6,7},{1,0},{3,2},{5,4},{7,6},{8,9},{10,11},{12,... | collective-permute-start | bytes 430088 | tf_op jit(solution)/shard_map/ppermute | solution.py:627
  21.8 7.4 %collective-permute-start.3 = (f32[280,128]{1,0:T(8,128)S(1)}, f32[280,128]{1,0:T(8,128)S(1)}, u32[]{:S(2)}, u32[]{:S(2)}) collective-permute-start(f32[280,128]{1,0:T(8,128)S(1)} %get-tuple-element.23), channel_id=1, source_target_pairs={{1,2},{3,4},{5,6},{2,1},{4,3},{6,5},{9,10},{11,12},{13,14},{10,9},... | collective-permute-start | bytes 430088 | tf_op jit(solution)/shard_map/ppermute | solution.py:627
  30.8 13.6 %all-to-all-start.1 = ((f32[32,2,128]{2,1,0:T(2,128)}), f32[32,2,128]{2,1,0:T(2,128)S(1)}, u32[]{:S(2)}, u32[]{:S(2)}) async-start(f32[32,2,128]{2,1,0:T(2,128)} %bitcast.6), calls=%async_computation.1 | async-start | bytes 65536 | tf_op jit(solution)/shard_map/all_to_all | solution.py:672

commit v3 on v2

--- a/solution.py
+++ b/solution.py
@@ -25,23 +25,18 @@
     return -(-count // unit) * unit
 
 
-def inverse_sinh(value):
-    magnitude = jnp.abs(value)
-    squared = magnitude * magnitude
-    positive = jnp.log1p(magnitude + squared / (1.0 + jnp.sqrt(1.0 + squared)))
-    return jnp.where(value < 0.0, -positive, positive)
-
-
 def friction_solve(shear, normal, shear_init, normal_init, state_var, slip_prev):
     shear_total = shear_init + shear
-    normal_eff = normal_init * (1.0 + 0.5 * jnp.tanh(normal))
+    strength = fric_a * (normal_init * (1.0 + 0.5 * jnp.tanh(normal)))
     growth = jnp.exp(state_var / fric_a) * 0.5
+    steep = strength * growth
     slip_now = slip_prev
     for newton_step in range(NEWTON_ITERS):
         scaled = growth * slip_now
-        misfit = shear_total - slip_now - fric_a * normal_eff * inverse_sinh(scaled)
-        slope_val = -1.0 - fric_a * normal_eff * growth / jnp.sqrt(1.0 + scaled * scaled)
-        slip_now = slip_now - misfit / slope_val
+        root = jnp.sqrt(1.0 + scaled * scaled)
+        positive = jnp.log(jnp.abs(scaled) + root)
+        misfit = shear_total - slip_now - strength * jnp.where(scaled < 0.0, -positive, positive)
+        slip_now = slip_now + misfit / (1.0 + steep / root)
     return slip_now
 
 
@@ -97,23 +92,22 @@
     return jnp.concatenate([ref[i : i + 1, :] for i in range(ref.shape[0])], axis=1)
 
 
-def star_apply(star_ref, moved_ref, basis, side, emit):
-    group = 3
+def star_group(star_ref, part_of, side, first, count):
+    totals = [None] * count
+    for inner in range(QUANT):
+        for axis_dir in range(DIMS):
+            part = part_of(inner, axis_dir)
+            for i in range(count):
+                at = (axis_dir * QUANT + first + i) * QUANT + inner
+                term = lane_row(star_ref, at, side) * part
+                totals[i] = term if totals[i] is None else totals[i] + term
+    return totals
+
+
+def star_apply(star_ref, part_of, side, emit, group=3):
     for first in range(0, QUANT, group):
-        totals = [None] * group
-        for inner in range(QUANT):
-            for axis_dir in range(DIMS):
-                part = moved_ref[
-                    inner,
-                    axis_dir * basis : (axis_dir + 1) * basis,
-                    side * LANES : (side + 1) * LANES,
-                ]
-                for i in range(group):
-                    at = (axis_dir * QUANT + first + i) * QUANT + inner
-                    term = lane_row(star_ref, at, side) * part
-                    totals[i] = term if totals[i] is None else totals[i] + term
-        for i in range(group):
-            emit(first + i, totals[i])
+        for i, total in enumerate(star_group(star_ref, part_of, side, first, group)):
+            emit(first + i, total)
 
 
 def flux_apply(flux_ref, which, values_of, face, side, totals):
@@ -250,7 +244,9 @@
     slot_most = max(2, 2 * faults // devices)
     slots = devices * slot_most
     sides_all = FACES * elems
-    left_q = (QUANT + 1) // 2
+    left_q = QUANT // 2
+    cut = up(basis // 2, SUB)
+    halo_rows = left_q * basis + cut
     depth = up(3 * basis, 16)
     turn_depth = up(3 * node_pad, 16)
     item_row = 4 * node_pad
@@ -264,13 +260,35 @@
     def odd_place():
         return lax.axis_index("row") % 2 == 1, lax.axis_index("col") % 2 == 1
 
-    def predict_kernel(ins, outs, moved_ref, piece_ref, table_ref):
-        kxi_at, part_at, item_at, fault_at, dofs_at, star_at, send_at = 0, 1, 2, 3, 7, 8, 9
+    def predict_kernel(ins, outs, table_ref, chosen_ref, *by_side):
+        moved_refs, piece_refs = by_side[:sides], by_side[sides:]
+        kxi_at, dofs_at, star_at, part_at, item_at, fault_at, send_at = 0, 1, 2, 3, 4, 5, 9
         proj_at, orient_at, near_at, code_at = range(10, 14)
         asked_at, slot_at, work_at, sends_at = 0, 1, 2, 3
         trace_table_at, turn_table_at, near_out, code_out = range(7, 11)
+        lanes_of = [slice(side * LANES, (side + 1) * LANES) for side in range(sides)]
         kxi_ref = ins[kxi_at]
         table_ref[...] = table(jnp.concatenate([kxi_ref[d].T for d in range(DIMS)], axis=0))
+        dofs_ref, work_ref = ins[dofs_at], outs[work_at]
+        for q in range(QUANT):
+            rows = slice(q * basis, (q + 1) * basis)
+            for side in range(sides):
+                start = dofs_ref[rows, lanes_of[side]]
+                work_ref[rows, lanes_of[side]] = time_step * start
+                piece_refs[side][q] = pieces(start)
+
+        def multiply(side):
+            for q in range(0, QUANT, 2):
+                quants = range(q, min(q + 2, QUANT))
+                right = jnp.concatenate([piece_refs[side][one] for one in quants], axis=1)
+                got = product(table_ref[...], right)
+                for i, one in enumerate(quants):
+                    moved_refs[side][one] = got[:, i * LANES : (i + 1) * LANES]
+
+        def part_of(side):
+            return lambda q, d: moved_refs[side][q, d * basis : (d + 1) * basis, :]
+
+        multiply(0)
         by_row = lax.broadcasted_iota(jnp.int32, (faults, faults), 0)
         by_lane = lax.broadcasted_iota(jnp.int32, (faults, faults), 1)
         across = ins[part_at][...]
@@ -281,7 +299,6 @@
         )
         place = across * slot_most + rank
         outs[slot_at][...] = place
-        outs.flush(slot_at)
         chosen = one_hot(0, slots, place)
         item = (ins[item_at][...] + 1).astype(f32)
         rows = [pad_rows(ins[fault_at + i][...], node_pad) for i in range(4)]
@@ -294,7 +311,6 @@
             preferred_element_type=f32,
         )
         outs.flush(asked_at)
-
         proj_ref, orient_ref = ins[proj_at], ins[orient_at]
         outs[trace_table_at][...] = table(
             jnp.concatenate([pad_rows(proj_ref[:, j, :], node_pad) for j in range(FACES)], axis=0)
@@ -313,31 +329,6 @@
             near < sides_all, near, near + ghosts * flip * (1 - 2 * (block % 2))
         )
         outs[code_out][...] = flat_row(ins[code_at])
-
-        dofs_ref, work_ref = ins[dofs_at], outs[work_at]
-        for q in range(QUANT):
-            start = dofs_ref[q * basis : (q + 1) * basis, :]
-            work_ref[q * basis : (q + 1) * basis, :] = time_step * start
-            piece_ref[q] = pieces(start)
-        star_ref = ins[star_at]
-
-        def advance(order_k, factor):
-            for q in range(QUANT):
-                moved_ref[q] = product(table_ref[...], piece_ref[q])
-            factor = factor * time_step / (order_k + 1).astype(f32)
-            for side in range(sides):
-                lanes = slice(side * LANES, (side + 1) * LANES)
-
-                def emit(p, value):
-                    piece_ref[p, :, lanes] = pieces(value)
-                    rows = slice(p * basis, (p + 1) * basis)
-                    work_ref[rows, lanes] = work_ref[rows, lanes] + factor * value
-
-                star_apply(star_ref, moved_ref, basis, side, emit)
-            return factor
-
-        lax.fori_loop(1, ORDER, advance, f32(time_step))
-        outs.flush(work_at)
         picks = ins[send_at][...]
         picks = jnp.concatenate([picks, picks], axis=1)
         order = [
@@ -347,19 +338,45 @@
             jnp.where(odd_col, picks[2:3], picks[3:4]),
         ]
         width = 2 * ghosts
-        chosen = jnp.concatenate([one_hot(0, elems, order[d]) for d in range(4)], axis=1)
-        low = lax.broadcasted_iota(jnp.int32, (basis, width), 1) < ghosts
-        got = []
-        for q in range(QUANT):
-            head, rest = split(work_ref[q * basis : (q + 1) * basis, :])
-            both = product(jnp.concatenate([head, rest], axis=0).astype(half), chosen)
-            got.append(both[:basis] + both[basis:])
+        for d in range(4):
+            chosen_ref[:, d * width : (d + 1) * width] = one_hot(0, elems, order[d])
+        star_ref = ins[star_at]
+
+        def advance(order_k, factor):
+            factor = factor * time_step / (order_k + 1).astype(f32)
+            for side in range(sides):
+                lanes = lanes_of[side]
+
+                def emit(p, value):
+                    piece_refs[side][p] = pieces(value)
+                    rows = slice(p * basis, (p + 1) * basis)
+                    work_ref[rows, lanes] = work_ref[rows, lanes] + factor * value
+
+                multiply((side + 1) % sides)
+                star_apply(star_ref, part_of(side), side, emit)
+            return factor
+
+        factor = lax.fori_loop(1, ORDER - 1, advance, f32(time_step))
+        factor = factor * (time_step / ORDER)
+
+        for side in range(sides):
+            lanes = lanes_of[side]
+
+            def emit_last(p, value):
+                rows = slice(p * basis, (p + 1) * basis)
+                work_ref[rows, lanes] = work_ref[rows, lanes] + factor * value
+
+            if side + 1 < sides:
+                multiply(side + 1)
+            star_apply(star_ref, part_of(side), side, emit_last)
+        heads, rests = split(work_ref[...])
+        both = product(jnp.concatenate([heads, rests], axis=0).astype(half), chosen_ref[...])
+        got = both[: QUANT * basis] + both[QUANT * basis :]
+        right = pad_rows(got[halo_rows:], halo_rows)
+        low = lax.broadcasted_iota(jnp.int32, (halo_rows, width), 1) < ghosts
         for d in range(4):
             lanes = slice(d * width, (d + 1) * width)
-            for q in range(left_q):
-                first = got[q][:, lanes]
-                second = got[q + left_q][:, lanes] if q + left_q < QUANT else first
-                outs[sends_at + d][q * basis : (q + 1) * basis, :] = jnp.where(low, first, second)
+            outs[sends_at + d][...] = jnp.where(low, got[:halo_rows, lanes], right[:, lanes])
 
     def asked_item(asked):
         return asked[item_row : item_row + 1, :].astype(jnp.int32) - 1
@@ -407,21 +424,29 @@
     def seen_across(
         got_refs, quants, trace_table, turn_table, near, code, seen_ref, chosen_ref, left_ref, emit
     ):
-        low = lax.broadcasted_iota(jnp.int32, (basis, 2 * ghosts), 1) < ghosts
+        def joined(first, second, begin, end):
+            low = lax.broadcasted_iota(jnp.int32, (end - begin, 2 * ghosts), 1) < ghosts
+            if end <= halo_rows:
+                rows = slice(begin, end)
+                return jnp.where(low, first[rows, :], pltpu.roll(second[rows, :], ghosts, 1))
+            rows = slice(begin - halo_rows, end - halo_rows)
+            return jnp.where(low, pltpu.roll(first[rows, :], ghosts, 1), second[rows, :])
+
+        def ghost_rows(first, second, begin, end):
+            if begin < halo_rows < end:
+                parts = [joined(first, second, begin, halo_rows), joined(first, second, halo_rows, end)]
+                return jnp.concatenate(parts, axis=0)
+            return joined(first, second, begin, end)
+
         for j in range(FACES):
             chosen_ref[j * ghost_all : (j + 1) * ghost_all, :] = one_hot(
                 sides_all + j * ghost_all, ghost_all, near
             )
         for at, q in enumerate(quants):
-            halves = []
-            for first, second in (got_refs[:2], got_refs[2:]):
-                if q < left_q:
-                    rows = slice(q * basis, (q + 1) * basis)
-                    a, b = first[rows, :], pltpu.roll(second[rows, :], ghosts, 1)
-                else:
-                    rows = slice((q - left_q) * basis, (q - left_q + 1) * basis)
-                    a, b = pltpu.roll(first[rows, :], ghosts, 1), second[rows, :]
-                halves.append(jnp.where(low, a, b))
+            halves = [
+                ghost_rows(first, second, q * basis, (q + 1) * basis)
+                for first, second in (got_refs[:2], got_refs[2:])
+            ]
             got = product(trace_table, pieces(jnp.concatenate(halves, axis=1)))
             for j in range(FACES):
                 head, rest = split(got[j * node_pad : (j + 1) * node_pad])
@@ -558,7 +583,12 @@
                 rows = slice(p * basis, (p + 1) * basis)
                 out_ref[rows, lanes] = dofs_ref[rows, lanes] + 0.25 * value
 
-            star_apply(star_ref, moved_ref, basis, side, emit)
+            star_apply(
+                star_ref,
+                lambda q, d: moved_ref[q, d * basis : (d + 1) * basis, lanes],
+                side,
+                emit,
+            )
         for p in range(QUANT):
             rows = slice(p * basis, (p + 1) * basis)
             out_ref[rows, :] = out_ref[rows, :] + 0.25 * product(lift_table, mixed_ref[p])
@@ -582,14 +612,14 @@
         "predict",
         [
             kxi,
+            dofs,
+            star,
             fault_part.reshape(1, faults),
             fault_item.reshape(1, faults),
             shear_init,
             normal_init,
             state_var,
             slip_prev,
-            dofs,
-            star,
             send_list,
             proj_rows,
             orient,
@@ -601,7 +631,7 @@
             ((1, faults), jnp.int32, "vmem"),
             (dofs.shape, f32, "vmem"),
         ]
-        + [((left_q * basis, 2 * ghosts), f32, "any")] * 4
+        + [((halo_rows, 2 * ghosts), f32, "any")] * 4
         + [
             ((FACES * node_pad, depth), half, "vmem"),
             ((TURNS * node_pad, turn_depth), half, "vmem"),
@@ -609,9 +639,10 @@
             ((1, sides_all), jnp.int32, "vmem"),
         ],
         scratch=(
-            vmem((QUANT, DIMS * basis, elems), f32),
-            vmem((QUANT, depth, elems), half),
             vmem((DIMS * basis, depth), half),
+            vmem((elems, 8 * ghosts), half),
+            *[vmem((QUANT, DIMS * basis, LANES), f32)] * sides,
+            *[vmem((QUANT, depth, LANES), half)] * sides,
         ),
         flops=5 * 2 * DIMS * basis * depth * QUANT * elems,
         moved=8_000_000,

time: 45.6 us -> 44.6 us (0.978)
  Pallas kernels: 22.2 us -> 21.3 us
    pallas_call x5, Pallas kernels: 22.2 us -> 21.3 us  [call(): pl.pallas_call(body, name=name, out_shape=shapes, in_specs=[pl.BlockSpec(...]
where the time goes in v3:
time: 44.6 us; the launch traced here: 44.4 us
  Pallas kernels  21.3 us (48%)
  starting transfers between devices  16.8 us (38%)
  waiting for transfers between devices  5.52 us (12%)
  between operations  0.74 us (2%)
    pallas_call x5, Pallas kernels, call(): pl.pallas_call(body, name=name, out_shape=shapes, in_specs=[pl.BlockSpec(...  21.3 us
    all_to_all x1, starting transfers between devices, per_device(): lax.all_to_all(asked.reshape(devices, slot_most, LANES), ('row', 'col'),...  7.3 us
    all_to_all x1, starting transfers between devices, per_device(): lax.all_to_all(back.reshape(devices, *chunk_shape), ('row', 'col'), split...  6.23 us
    all_to_all x1, waiting for transfers between devices, per_device(): lax.all_to_all(asked.reshape(devices, slot_most, LANES), ('row', 'col'),...  4.92 us
    ppermute x4, starting transfers between devices, swapped(): return lax.ppermute(values, axis, pairs + [(b, a) for a, b in pairs])  3.23 us
  transfers between devices with their start and end apart: 6, of which 2 were waited for; matrix products, arithmetic and copies ran while one was open for 0% of the time, Pallas kernels for 19%

profile of v3, /device:TPU:0, one launch (start us, length us, event | category | flops | bytes accessed | tf_op | source)
XLA Modules:
  0.0 44.4 jit_solution(9033080749080411502)
XLA Ops:
  0.6 10.5 %predict.1 = (f32[256,128]{1,0:T(8,128)}, s32[1,128]{1,0:T(1,128)S(1)}, f32[504,256]{1,0:T(8,128)S(1)}, f32[256,128]{1,0:T(8,128)S(1)}, f32[256,128]{1,0:T(8,128...) custom-call(f32[3,56,56]{2,1,0:T(8,128)} %refs_13_.3, ...), custom_call_target="tpu_custom_call" | custom-call | flops 681246720 | bytes 8000000 | tf_op jit(solution)/shard_map/predict/pallas_call | solution.py:200
  11.1 7.3 %all-to-all-start = ((f32[32,8,128]{2,1,0:T(8,128)}), f32[32,8,128]{2,1,0:T(8,128)S(1)}, u32[]{:S(2)}, u32[]{:S(2)}) async-start(f32[32,8,128]{2,1,0:T(8,128)} %bitcast.12), calls=%async_computation | async-start | bytes 262144 | tf_op jit(solution)/shard_map/all_to_all | solution.py:652
  18.4 1.8 %collective-permute-start = (f32[256,128]{1,0:T(8,128)S(1)}, f32[256,128]{1,0:T(8,128)S(1)}, u32[]{:S(2)}, u32[]{:S(2)}) collective-permute-start(f32[256,128]{1,0:T(8,128)S(1)} %get-tuple-element.20), channel_id=1, source_target_pairs={{0,8},{16,24},{8,0},{24,16},{1,9},{17,25},{9,1},{25,17},{2,10},{18... | collective-permute-start | bytes 393224 | tf_op jit(solution)/shard_map/ppermute | solution.py:658
  20.3 0.7 %collective-permute-start.1 = (f32[256,128]{1,0:T(8,128)S(1)}, f32[256,128]{1,0:T(8,128)S(1)}, u32[]{:S(2)}, u32[]{:S(2)}) collective-permute-start(f32[256,128]{1,0:T(8,128)S(1)} %get-tuple-element.21), channel_id=1, source_target_pairs={{8,16},{16,8},{9,17},{17,9},{10,18},{18,10},{11,19},{19,11},{12,20... | collective-permute-start | bytes 393224 | tf_op jit(solution)/shard_map/ppermute | solution.py:658
  20.9 0.1 collective-permute-start.2
  21.0 0.7 %collective-permute-start.3 = (f32[256,128]{1,0:T(8,128)S(1)}, f32[256,128]{1,0:T(8,128)S(1)}, u32[]{:S(2)}, u32[]{:S(2)}) collective-permute-start(f32[256,128]{1,0:T(8,128)S(1)} %get-tuple-element.23), channel_id=1, source_target_pairs={{1,2},{3,4},{5,6},{2,1},{4,3},{6,5},{9,10},{11,12},{13,14},{10,9},... | collective-permute-start | bytes 393224 | tf_op jit(solution)/shard_map/ppermute | solution.py:658
  21.7 4.9 %all-to-all-done = f32[32,8,128]{2,1,0:T(8,128)S(1)} async-done(((f32[32,8,128]{2,1,0:T(8,128)}), f32[32,8,128]{2,1,0:T(8,128)S(1)}, u32[]{:S(2)}, u32[]{:S(2)}) %all-to-all-start) | async-done | bytes 131104 | tf_op jit(solution)/shard_map/all_to_all | solution.py:652
  26.6 1.7 %local_terms.1 = (bf16[432,1024]{1,0:T(8,128)(2,1)S(1)}, f32[48,256]{1,0:T(8,128)S(1)}, bf16[144,256]{1,0:T(8,128)(2,1)S(1)}, s32[1,256]{1,0:T(1,128)S(1)}, s32[1,256]{1,0:T(1,128)S(1)}) custom-call(s32[1,1024]{1,0:T(1,128)S(1)} %get-tuple-element.26.refs_0_.refs_6_, bf16[96,176]{1,0:T(8,128)(2,1)S(1)} %get-tuple-element.24.refs_1_.refs_4_, ...), custom_call_target="tpu_custom_call" | custom-call | flops 905969664 | bytes 8000000 | tf_op jit(solution)/shard_map/local_terms/pallas_call | solution.py:200
  28.4 0.0 collective-permute-done.refs_0_
  28.4 0.0 collective-permute-done.1.refs_1_
  28.4 0.0 collective-permute-done.2.refs_2_
  28.4 0.0 collective-permute-done.3.refs_3_
  28.4 1.6 %friction.1 = (f32[64,128]{1,0:T(8,128)}, f32[24,256]{1,0:T(8,128)S(1)}) custom-call(f32[256,128]{1,0:T(8,128)S(1)} %collective-permute-done.refs_0_, f32[256,128]{1,0:T(8,128)S(1)} %collective-permute-done.1.refs_1_, f32[256,128]{1,0:T(8,128)S(1)} %collective-permute-done.2.refs_2_, f32[256,128]{1,0:T(8,128)S(1)} %collective-permute-done.3.refs_3_, ...), custom_call_target="tpu_custom_call" | custom-call | flops 75497472 | bytes 4000000 | tf_op jit(solution)/shard_map/friction/pallas_call | solution.py:200
  30.0 6.2 %all-to-all-start.1 = ((f32[32,2,128]{2,1,0:T(2,128)}), f32[32,2,128]{2,1,0:T(2,128)S(1)}, u32[]{:S(2)}, u32[]{:S(2)}) async-start(f32[32,2,128]{2,1,0:T(2,128)} %bitcast.6), calls=%async_computation.1 | async-start | bytes 65536 | tf_op jit(solution)/shard_map/all_to_all | solution.py:703
  36.3 6.6 %final_terms.1 = f32[504,256]{1,0:T(8,128)} custom-call(f32[256,128]{1,0:T(8,128)S(1)} %collective-permute-done.refs_0_, f32[256,128]{1,0:T(8,128)S(1)} %collective-permute-done.1.refs_1_, f32[256,128]{1,0:T(8,128)S(1)} %collective-permute-done.2.refs_2_, f32[256,128]{1,0:T(8,128)S(1)} %collective-permute-done.3.refs_3_, ...), custom_call_target="tpu_custom_call" | custom-call | flops 905969664 | bytes 8000000 | tf_op jit(solution)/shard_map/final_terms/pallas_call | solution.py:200
  42.9 0.6 %all-to-all-done.1 = f32[32,2,128]{2,1,0:T(2,128)S(1)} async-done(((f32[32,2,128]{2,1,0:T(2,128)}), f32[32,2,128]{2,1,0:T(2,128)S(1)}, u32[]{:S(2)}, u32[]{:S(2)}) %all-to-all-start.1) | async-done | bytes 32800 | tf_op jit(solution)/shard_map/all_to_all | solution.py:703
  43.5 0.9 %fault_return.1 = f32[21,128]{1,0:T(8,128)} custom-call(s32[1,128]{1,0:T(1,128)S(1)} %get-tuple-element.36.refs_0_, f32[64,128]{1,0:T(8,128)S(1)} %bitcast.11), custom_call_target="tpu_custom_call" | custom-call | flops 3145728 | bytes 200000 | tf_op jit(solution)/shard_map/fault_return/pallas_call | solution.py:200
Async XLA Ops:
  11.1 15.5 %all-to-all-start = ((f32[32,8,128]{2,1,0:T(8,128)}), f32[32,8,128]{2,1,0:T(8,128)S(1)}, u32[]{:S(2)}, u32[]{:S(2)}) async-start(f32[32,8,128]{2,1,0:T(8,128)} %bitcast.12), calls=%async_computation | async-start | bytes 262144 | tf_op jit(solution)/shard_map/all_to_all | solution.py:652
  18.4 9.9 %collective-permute-start = (f32[256,128]{1,0:T(8,128)S(1)}, f32[256,128]{1,0:T(8,128)S(1)}, u32[]{:S(2)}, u32[]{:S(2)}) collective-permute-start(f32[256,128]{1,0:T(8,128)S(1)} %get-tuple-element.20), channel_id=1, source_target_pairs={{0,8},{16,24},{8,0},{24,16},{1,9},{17,25},{9,1},{25,17},{2,10},{18... | collective-permute-start | bytes 393224 | tf_op jit(solution)/shard_map/ppermute | solution.py:658
  20.3 8.1 %collective-permute-start.1 = (f32[256,128]{1,0:T(8,128)S(1)}, f32[256,128]{1,0:T(8,128)S(1)}, u32[]{:S(2)}, u32[]{:S(2)}) collective-permute-start(f32[256,128]{1,0:T(8,128)S(1)} %get-tuple-element.21), channel_id=1, source_target_pairs={{8,16},{16,8},{9,17},{17,9},{10,18},{18,10},{11,19},{19,11},{12,20... | collective-permute-start | bytes 393224 | tf_op jit(solution)/shard_map/ppermute | solution.py:658
  20.9 7.5 %collective-permute-start.2 = (f32[256,128]{1,0:T(8,128)S(1)}, f32[256,128]{1,0:T(8,128)S(1)}, u32[]{:S(2)}, u32[]{:S(2)}) collective-permute-start(f32[256,128]{1,0:T(8,128)S(1)} %get-tuple-element.22), channel_id=1, source_target_pairs={{0,1},{2,3},{4,5},{6,7},{1,0},{3,2},{5,4},{7,6},{8,9},{10,11},{12,... | collective-permute-start | bytes 393224 | tf_op jit(solution)/shard_map/ppermute | solution.py:658
  21.0 7.4 %collective-permute-start.3 = (f32[256,128]{1,0:T(8,128)S(1)}, f32[256,128]{1,0:T(8,128)S(1)}, u32[]{:S(2)}, u32[]{:S(2)}) collective-permute-start(f32[256,128]{1,0:T(8,128)S(1)} %get-tuple-element.23), channel_id=1, source_target_pairs={{1,2},{3,4},{5,6},{2,1},{4,3},{6,5},{9,10},{11,12},{13,14},{10,9},... | collective-permute-start | bytes 393224 | tf_op jit(solution)/shard_map/ppermute | solution.py:658
  30.0 13.5 %all-to-all-start.1 = ((f32[32,2,128]{2,1,0:T(2,128)}), f32[32,2,128]{2,1,0:T(2,128)S(1)}, u32[]{:S(2)}, u32[]{:S(2)}) async-start(f32[32,2,128]{2,1,0:T(2,128)} %bitcast.6), calls=%async_computation.1 | async-start | bytes 65536 | tf_op jit(solution)/shard_map/all_to_all | solution.py:703

commit v4 on v3

--- a/solution.py
+++ b/solution.py
@@ -263,9 +263,7 @@
     def predict_kernel(ins, outs, table_ref, chosen_ref, *by_side):
         moved_refs, piece_refs = by_side[:sides], by_side[sides:]
         kxi_at, dofs_at, star_at, part_at, item_at, fault_at, send_at = 0, 1, 2, 3, 4, 5, 9
-        proj_at, orient_at, near_at, code_at = range(10, 14)
         asked_at, slot_at, work_at, sends_at = 0, 1, 2, 3
-        trace_table_at, turn_table_at, near_out, code_out = range(7, 11)
         lanes_of = [slice(side * LANES, (side + 1) * LANES) for side in range(sides)]
         kxi_ref = ins[kxi_at]
         table_ref[...] = table(jnp.concatenate([kxi_ref[d].T for d in range(DIMS)], axis=0))
@@ -311,24 +309,7 @@
             preferred_element_type=f32,
         )
         outs.flush(asked_at)
-        proj_ref, orient_ref = ins[proj_at], ins[orient_at]
-        outs[trace_table_at][...] = table(
-            jnp.concatenate([pad_rows(proj_ref[:, j, :], node_pad) for j in range(FACES)], axis=0)
-        )
-        outs[turn_table_at][...] = table(
-            jnp.concatenate(
-                [pad_lanes(pad_rows(orient_ref[t].T, node_pad), node_pad) for t in range(TURNS)],
-                axis=0,
-            )
-        )
         odd_row, odd_col = odd_place()
-        near = flat_row(ins[near_at])
-        block = (near // ghosts) % 4
-        flip = jnp.where(block < 2, jnp.where(odd_row, 0, 1), jnp.where(odd_col, 0, 1))
-        outs[near_out][...] = jnp.where(
-            near < sides_all, near, near + ghosts * flip * (1 - 2 * (block % 2))
-        )
-        outs[code_out][...] = flat_row(ins[code_at])
         picks = ins[send_at][...]
         picks = jnp.concatenate([picks, picks], axis=1)
         order = [
@@ -382,9 +363,14 @@
         return asked[item_row : item_row + 1, :].astype(jnp.int32) - 1
 
     def local_kernel(ins, outs, left_ref, chosen_ref, wanted_ref):
-        near_at, trace_table_at, work_at, code_at, asked_at = range(5)
+        proj_at, near_at, work_at, orient_at, code_at, asked_at = range(6)
         seen_at, fric_at, slot_seen_at, slot_near_at, slot_code_at = range(5)
-        trace_table = ins[trace_table_at][...]
+        trace_table_at, turn_table_at, near_out, code_out = range(5, 9)
+        proj_ref = ins[proj_at]
+        trace_table = table(
+            jnp.concatenate([pad_rows(proj_ref[:, j, :], node_pad) for j in range(FACES)], axis=0)
+        )
+        outs[trace_table_at][...] = trace_table
         work_ref = ins[work_at]
         kept = {}
         for q in range(QUANT):
@@ -396,7 +382,21 @@
                 left_ref[q * pair : (q + 1) * pair, j * elems : (j + 1) * elems] = jnp.concatenate(
                     [head, rest], axis=0
                 ).astype(half)
-        near = ins[near_at][...]
+        near = flat_row(ins[near_at])
+        odd_row, odd_col = odd_place()
+        block = (near // ghosts) % 4
+        flip = jnp.where(block < 2, jnp.where(odd_row, 0, 1), jnp.where(odd_col, 0, 1))
+        near = jnp.where(near < sides_all, near, near + ghosts * flip * (1 - 2 * (block % 2)))
+        outs[near_out][...] = near
+        code = flat_row(ins[code_at])
+        outs[code_out][...] = code
+        orient_ref = ins[orient_at]
+        outs[turn_table_at][...] = table(
+            jnp.concatenate(
+                [pad_lanes(pad_rows(orient_ref[t].T, node_pad), node_pad) for t in range(TURNS)],
+                axis=0,
+            )
+        )
         for j in range(FACES):
             chosen_ref[j * elems : (j + 1) * elems, :] = one_hot(j * elems, elems, near)
         outs[seen_at][...] = product(left_ref[...], chosen_ref[...]).astype(half)
@@ -409,7 +409,7 @@
             shear.append(0.5 * (kept[3][rows] + kept[6][rows]))
             normal.append(0.5 * kept[0][rows])
         rows = [*split(jnp.concatenate(shear, axis=1)), *split(jnp.concatenate(normal, axis=1))]
-        rows += [near_head, near_rest, ins[code_at][...].astype(f32)]
+        rows += [near_head, near_rest, code.astype(f32)]
         rows = jnp.concatenate(rows, axis=0)
         taken = product(pad_rows(rows, up(rows.shape[0], 16)).astype(half), wanted_ref[...])
         outs[fric_at][:node_pad, :] = taken[:node_pad] + taken[node_pad:pair]
@@ -607,7 +607,7 @@
     vmem = pltpu.VMEM
     proj_rows = jnp.transpose(face_proj, (2, 0, 1))
     lift_rows = jnp.transpose(face_lift, (1, 0, 2))
-    *first_outs, trace_table, turn_table, near, code = call(
+    asked, slot_of, work, *sends = call(
         predict_kernel,
         "predict",
         [
@@ -621,23 +621,13 @@
             state_var,
             slip_prev,
             send_list,
-            proj_rows,
-            orient,
-            neighbour,
-            orient_code,
         ],
         [
             ((slots, LANES), f32, "hbm"),
             ((1, faults), jnp.int32, "vmem"),
             (dofs.shape, f32, "vmem"),
         ]
-        + [((halo_rows, 2 * ghosts), f32, "any")] * 4
-        + [
-            ((FACES * node_pad, depth), half, "vmem"),
-            ((TURNS * node_pad, turn_depth), half, "vmem"),
-            ((1, sides_all), jnp.int32, "vmem"),
-            ((1, sides_all), jnp.int32, "vmem"),
-        ],
+        + [((halo_rows, 2 * ghosts), f32, "any")] * 4,
         scratch=(
             vmem((DIMS * basis, depth), half),
             vmem((elems, 8 * ghosts), half),
@@ -648,7 +638,6 @@
         moved=8_000_000,
     )
 
-    asked, slot_of, work, *sends = first_outs
     asked = lax.all_to_all(
         asked.reshape(devices, slot_most, LANES), ("row", "col"), split_axis=0, concat_axis=0, tiled=True
     ).reshape(slots, LANES)
@@ -664,16 +653,20 @@
         swapped(sends[3], "col", 1),
     ]
 
-    seen, fric, slot_seen, slot_near, slot_code = call(
+    seen, fric, slot_seen, slot_near, slot_code, trace_table, turn_table, near, code = call(
         local_kernel,
         "local_terms",
-        [Kept(one) for one in (near, trace_table, work, code, asked)],
+        [proj_rows, neighbour, Kept(work), orient, orient_code, Kept(asked)],
         [
             ((QUANT * pair, sides_all), half, "vmem"),
             ((pair, slots), f32, "vmem"),
             ((len(first_q) * pair, slots), half, "vmem"),
             ((1, slots), jnp.int32, "vmem"),
             ((1, slots), jnp.int32, "vmem"),
+            ((FACES * node_pad, depth), half, "vmem"),
+            ((TURNS * node_pad, turn_depth), half, "vmem"),
+            ((1, sides_all), jnp.int32, "vmem"),
+            ((1, sides_all), jnp.int32, "vmem"),
         ],
         scratch=(
             vmem((QUANT * pair, sides_all), half),

time: 44.6 us -> 44.4 us (level)
  starting transfers between devices: 16.8 us -> 15.7 us
  Pallas kernels: 21.3 us -> 22.1 us
    all_to_all x1, starting transfers between devices: 6.23 us -> 5.17 us  [per_device(): lax.all_to_all(back.reshape(devices, *chunk_shape), ('row', 'col'), split...]
    pallas_call x5, Pallas kernels: 21.3 us -> 22.1 us  [call(): pl.pallas_call(body, name=name, out_shape=shapes, in_specs=[pl.BlockSpec(...]
  transfers between devices with their start and end apart: 6 -> 6, of which waited for: 2 -> 2; matrix products, arithmetic and copies ran while one was open for 0% -> 0% of each run, Pallas kernels for 19% -> 21%
where the time goes in v4:
time: 44.4 us; the launch traced here: 44.1 us
  Pallas kernels  22.1 us (50%)
  starting transfers between devices  15.7 us (35%)
  waiting for transfers between devices  5.52 us (12%)
  between operations  0.74 us (2%)
    pallas_call x5, Pallas kernels, call(): pl.pallas_call(body, name=name, out_shape=shapes, in_specs=[pl.BlockSpec(...  22.1 us
    all_to_all x1, starting transfers between devices, per_device(): lax.all_to_all(asked.reshape(devices, slot_most, LANES), ('row', 'col'),...  7.3 us
    all_to_all x1, starting transfers between devices, per_device(): lax.all_to_all(back.reshape(devices, *chunk_shape), ('row', 'col'), split...  5.17 us
    all_to_all x1, waiting for transfers between devices, per_device(): lax.all_to_all(asked.reshape(devices, slot_most, LANES), ('row', 'col'),...  4.92 us
    ppermute x4, starting transfers between devices, swapped(): return lax.ppermute(values, axis, pairs + [(b, a) for a, b in pairs])  3.23 us
  transfers between devices with their start and end apart: 6, of which 2 were waited for; matrix products, arithmetic and copies ran while one was open for 0% of the time, Pallas kernels for 21%

profile of v4, /device:TPU:0, one launch (start us, length us, event | category | flops | bytes accessed | tf_op | source)
XLA Modules:
  0.0 44.1 jit_solution(12499663829262107706)
XLA Ops:
  0.6 10.2 %predict.1 = (f32[256,128]{1,0:T(8,128)}, s32[1,128]{1,0:T(1,128)S(1)}, f32[504,256]{1,0:T(8,128)S(1)}, f32[256,128]{1,0:T(8,128)S(1)}, f32[256,128]{1,0:T(8,128...) custom-call(f32[3,56,56]{2,1,0:T(8,128)} %refs_13_.1, f32[504,256]{1,0:T(8,128)} %refs_16_.1, f32[243,256]{1,0:T(8,128)} %refs_15_.1, ...), custom_call_target="tpu_custom_call" | custom-call | flops 681246720 | bytes 8000000 | tf_op jit(solution)/shard_map/predict/pallas_call | solution.py:200
  10.8 7.3 %all-to-all-start = ((f32[32,8,128]{2,1,0:T(8,128)}), f32[32,8,128]{2,1,0:T(8,128)S(1)}, u32[]{:S(2)}, u32[]{:S(2)}) async-start(f32[32,8,128]{2,1,0:T(8,128)} %bitcast.12), calls=%async_computation | async-start | bytes 262144 | tf_op jit(solution)/shard_map/all_to_all | solution.py:641
  18.1 1.8 %collective-permute-start = (f32[256,128]{1,0:T(8,128)S(1)}, f32[256,128]{1,0:T(8,128)S(1)}, u32[]{:S(2)}, u32[]{:S(2)}) collective-permute-start(f32[256,128]{1,0:T(8,128)S(1)} %get-tuple-element.20), channel_id=1, source_target_pairs={{0,8},{16,24},{8,0},{24,16},{1,9},{17,25},{9,1},{25,17},{2,10},{18... | collective-permute-start | bytes 393224 | tf_op jit(solution)/shard_map/ppermute | solution.py:647
  20.0 0.7 %collective-permute-start.1 = (f32[256,128]{1,0:T(8,128)S(1)}, f32[256,128]{1,0:T(8,128)S(1)}, u32[]{:S(2)}, u32[]{:S(2)}) collective-permute-start(f32[256,128]{1,0:T(8,128)S(1)} %get-tuple-element.21), channel_id=1, source_target_pairs={{8,16},{16,8},{9,17},{17,9},{10,18},{18,10},{11,19},{19,11},{12,20... | collective-permute-start | bytes 393224 | tf_op jit(solution)/shard_map/ppermute | solution.py:647
  20.6 0.1 collective-permute-start.2
  20.7 0.7 %collective-permute-start.3 = (f32[256,128]{1,0:T(8,128)S(1)}, f32[256,128]{1,0:T(8,128)S(1)}, u32[]{:S(2)}, u32[]{:S(2)}) collective-permute-start(f32[256,128]{1,0:T(8,128)S(1)} %get-tuple-element.23), channel_id=1, source_target_pairs={{1,2},{3,4},{5,6},{2,1},{4,3},{6,5},{9,10},{11,12},{13,14},{10,9},... | collective-permute-start | bytes 393224 | tf_op jit(solution)/shard_map/ppermute | solution.py:647
  21.4 4.9 %all-to-all-done = f32[32,8,128]{2,1,0:T(8,128)S(1)} async-done(((f32[32,8,128]{2,1,0:T(8,128)}), f32[32,8,128]{2,1,0:T(8,128)S(1)}, u32[]{:S(2)}, u32[]{:S(2)}) %all-to-all-start) | async-done | bytes 131104 | tf_op jit(solution)/shard_map/all_to_all | solution.py:641
  26.3 2.8 %local_terms.1 = (bf16[432,1024]{1,0:T(8,128)(2,1)S(1)}, f32[48,256]{1,0:T(8,128)S(1)}, bf16[144,256]{1,0:T(8,128)(2,1)S(1)}, s32[1,256]{1,0:T(1,128)S(1)}, s32[...) custom-call(f32[21,4,56]{2,1,0:T(4,128)} %bitcast.14, ...), custom_call_target="tpu_custom_call" | custom-call | flops 905969664 | bytes 8000000 | tf_op jit(solution)/shard_map/local_terms/pallas_call | solution.py:200
  29.1 0.0 collective-permute-done.refs_0_
  29.1 0.0 collective-permute-done.1.refs_1_
  29.2 0.0 collective-permute-done.2.refs_2_
  29.2 0.0 collective-permute-done.3.refs_3_
  29.2 1.6 %friction.1 = (f32[64,128]{1,0:T(8,128)}, f32[24,256]{1,0:T(8,128)S(1)}) custom-call(f32[256,128]{1,0:T(8,128)S(1)} %collective-permute-done.refs_0_, f32[256,128]{1,0:T(8,128)S(1)} %collective-permute-done.1.refs_1_, f32[256,128]{1,0:T(8,128)S(1)} %collective-permute-done.2.refs_2_, f32[256,128]{1,0:T(8,128)S(1)} %collective-permute-done.3.refs_3_, ...), custom_call_target="tpu_custom_call" | custom-call | flops 75497472 | bytes 4000000 | tf_op jit(solution)/shard_map/friction/pallas_call | solution.py:200
  30.8 5.2 %all-to-all-start.1 = ((f32[32,2,128]{2,1,0:T(2,128)}), f32[32,2,128]{2,1,0:T(2,128)S(1)}, u32[]{:S(2)}, u32[]{:S(2)}) async-start(f32[32,2,128]{2,1,0:T(2,128)} %bitcast.6), calls=%async_computation.1 | async-start | bytes 65536 | tf_op jit(solution)/shard_map/all_to_all | solution.py:696
  36.0 6.6 %final_terms.1 = f32[504,256]{1,0:T(8,128)} custom-call(f32[256,128]{1,0:T(8,128)S(1)} %collective-permute-done.refs_0_, f32[256,128]{1,0:T(8,128)S(1)} %collective-permute-done.1.refs_1_, f32[256,128]{1,0:T(8,128)S(1)} %collective-permute-done.2.refs_2_, f32[256,128]{1,0:T(8,128)S(1)} %collective-permute-done.3.refs_3_, ...), custom_call_target="tpu_custom_call" | custom-call | flops 905969664 | bytes 8000000 | tf_op jit(solution)/shard_map/final_terms/pallas_call | solution.py:200
  42.6 0.6 %all-to-all-done.1 = f32[32,2,128]{2,1,0:T(2,128)S(1)} async-done(((f32[32,2,128]{2,1,0:T(2,128)}), f32[32,2,128]{2,1,0:T(2,128)S(1)}, u32[]{:S(2)}, u32[]{:S(2)}) %all-to-all-start.1) | async-done | bytes 32800 | tf_op jit(solution)/shard_map/all_to_all | solution.py:696
  43.2 0.9 %fault_return.1 = f32[21,128]{1,0:T(8,128)} custom-call(s32[1,128]{1,0:T(1,128)S(1)} %get-tuple-element.36.refs_0_, f32[64,128]{1,0:T(8,128)S(1)} %bitcast.11), custom_call_target="tpu_custom_call" | custom-call | flops 3145728 | bytes 200000 | tf_op jit(solution)/shard_map/fault_return/pallas_call | solution.py:200
Async XLA Ops:
  10.8 15.5 %all-to-all-start = ((f32[32,8,128]{2,1,0:T(8,128)}), f32[32,8,128]{2,1,0:T(8,128)S(1)}, u32[]{:S(2)}, u32[]{:S(2)}) async-start(f32[32,8,128]{2,1,0:T(8,128)} %bitcast.12), calls=%async_computation | async-start | bytes 262144 | tf_op jit(solution)/shard_map/all_to_all | solution.py:641
  18.1 11.0 %collective-permute-start = (f32[256,128]{1,0:T(8,128)S(1)}, f32[256,128]{1,0:T(8,128)S(1)}, u32[]{:S(2)}, u32[]{:S(2)}) collective-permute-start(f32[256,128]{1,0:T(8,128)S(1)} %get-tuple-element.20), channel_id=1, source_target_pairs={{0,8},{16,24},{8,0},{24,16},{1,9},{17,25},{9,1},{25,17},{2,10},{18... | collective-permute-start | bytes 393224 | tf_op jit(solution)/shard_map/ppermute | solution.py:647
  20.0 9.2 %collective-permute-start.1 = (f32[256,128]{1,0:T(8,128)S(1)}, f32[256,128]{1,0:T(8,128)S(1)}, u32[]{:S(2)}, u32[]{:S(2)}) collective-permute-start(f32[256,128]{1,0:T(8,128)S(1)} %get-tuple-element.21), channel_id=1, source_target_pairs={{8,16},{16,8},{9,17},{17,9},{10,18},{18,10},{11,19},{19,11},{12,20... | collective-permute-start | bytes 393224 | tf_op jit(solution)/shard_map/ppermute | solution.py:647
  20.6 8.5 %collective-permute-start.2 = (f32[256,128]{1,0:T(8,128)S(1)}, f32[256,128]{1,0:T(8,128)S(1)}, u32[]{:S(2)}, u32[]{:S(2)}) collective-permute-start(f32[256,128]{1,0:T(8,128)S(1)} %get-tuple-element.22), channel_id=1, source_target_pairs={{0,1},{2,3},{4,5},{6,7},{1,0},{3,2},{5,4},{7,6},{8,9},{10,11},{12,... | collective-permute-start | bytes 393224 | tf_op jit(solution)/shard_map/ppermute | solution.py:647
  20.7 8.4 %collective-permute-start.3 = (f32[256,128]{1,0:T(8,128)S(1)}, f32[256,128]{1,0:T(8,128)S(1)}, u32[]{:S(2)}, u32[]{:S(2)}) collective-permute-start(f32[256,128]{1,0:T(8,128)S(1)} %get-tuple-element.23), channel_id=1, source_target_pairs={{1,2},{3,4},{5,6},{2,1},{4,3},{6,5},{9,10},{11,12},{13,14},{10,9},... | collective-permute-start | bytes 393224 | tf_op jit(solution)/shard_map/ppermute | solution.py:647
  30.8 12.4 %all-to-all-start.1 = ((f32[32,2,128]{2,1,0:T(2,128)}), f32[32,2,128]{2,1,0:T(2,128)S(1)}, u32[]{:S(2)}, u32[]{:S(2)}) async-start(f32[32,2,128]{2,1,0:T(2,128)} %bitcast.6), calls=%async_computation.1 | async-start | bytes 65536 | tf_op jit(solution)/shard_map/all_to_all | solution.py:696

commit v5 on v4

--- a/solution.py
+++ b/solution.py
@@ -597,11 +597,12 @@
         place = ins[0][...]
         held = ins[1][...].T
         rows = slots // per_row
-        got = jnp.zeros((pair, faults), f32)
+        lefts, picked = [], []
         for k in range(per_row):
             head, rest = split(held[k * slot_lanes : k * slot_lanes + node_pad])
-            chosen = one_hot(0, rows, jnp.where(place % per_row == k, place // per_row, -1))
-            got = got + product(jnp.concatenate([head, rest], axis=0).astype(half), chosen)
+            lefts.append(jnp.concatenate([head, rest], axis=0))
+            picked.append(one_hot(0, rows, jnp.where(place % per_row == k, place // per_row, -1)))
+        got = product(jnp.concatenate(lefts, axis=1).astype(half), jnp.concatenate(picked, axis=0))
         outs[0][...] = (got[:node_pad] + got[node_pad:])[:nodes]
 
     vmem = pltpu.VMEM

time: 44.4 us -> 44.4 us (level)
  no operation moved by 1% of the time
where the time goes in v5:
time: 44.4 us; the launch traced here: 44.1 us
  Pallas kernels  22.2 us (50%)
  starting transfers between devices  15.7 us (35%)
  waiting for transfers between devices  5.52 us (12%)
  between operations  0.74 us (2%)
    pallas_call x5, Pallas kernels, call(): pl.pallas_call(body, name=name, out_shape=shapes, in_specs=[pl.BlockSpec(...  22.2 us
    all_to_all x1, starting transfers between devices, per_device(): lax.all_to_all(asked.reshape(devices, slot_most, LANES), ('row', 'col'),...  7.3 us
    all_to_all x1, starting transfers between devices, per_device(): lax.all_to_all(back.reshape(devices, *chunk_shape), ('row', 'col'), split...  5.17 us
    all_to_all x1, waiting for transfers between devices, per_device(): lax.all_to_all(asked.reshape(devices, slot_most, LANES), ('row', 'col'),...  4.92 us
    ppermute x4, starting transfers between devices, swapped(): return lax.ppermute(values, axis, pairs + [(b, a) for a, b in pairs])  3.23 us
  transfers between devices with their start and end apart: 6, of which 2 were waited for; matrix products, arithmetic and copies ran while one was open for 0% of the time, Pallas kernels for 21%

profile of v5, /device:TPU:0, one launch (start us, length us, event | category | flops | bytes accessed | tf_op | source)
XLA Modules:
  0.0 44.1 jit_solution(10257361329894293256)
XLA Ops:
  0.6 10.2 %predict.1 = (f32[256,128]{1,0:T(8,128)}, s32[1,128]{1,0:T(1,128)S(1)}, f32[504,256]{1,0:T(8,128)S(1)}, f32[256,128]{1,0:T(8,128)S(1)}, f32[256,128]{1,0:T(8,128...) custom-call(f32[3,56,56]{2,1,0:T(8,128)} %refs_13_.1, f32[504,256]{1,0:T(8,128)} %refs_16_.1, f32[243,256]{1,0:T(8,128)} %refs_15_.1, ...), custom_call_target="tpu_custom_call" | custom-call | flops 681246720 | bytes 8000000 | tf_op jit(solution)/shard_map/predict/pallas_call | solution.py:200
  10.8 7.3 %all-to-all-start = ((f32[32,8,128]{2,1,0:T(8,128)}), f32[32,8,128]{2,1,0:T(8,128)S(1)}, u32[]{:S(2)}, u32[]{:S(2)}) async-start(f32[32,8,128]{2,1,0:T(8,128)} %bitcast.12), calls=%async_computation | async-start | bytes 262144 | tf_op jit(solution)/shard_map/all_to_all | solution.py:642
  18.1 1.8 %collective-permute-start = (f32[256,128]{1,0:T(8,128)S(1)}, f32[256,128]{1,0:T(8,128)S(1)}, u32[]{:S(2)}, u32[]{:S(2)}) collective-permute-start(f32[256,128]{1,0:T(8,128)S(1)} %get-tuple-element.20), channel_id=1, source_target_pairs={{0,8},{16,24},{8,0},{24,16},{1,9},{17,25},{9,1},{25,17},{2,10},{18... | collective-permute-start | bytes 393224 | tf_op jit(solution)/shard_map/ppermute | solution.py:648
  20.0 0.7 %collective-permute-start.1 = (f32[256,128]{1,0:T(8,128)S(1)}, f32[256,128]{1,0:T(8,128)S(1)}, u32[]{:S(2)}, u32[]{:S(2)}) collective-permute-start(f32[256,128]{1,0:T(8,128)S(1)} %get-tuple-element.21), channel_id=1, source_target_pairs={{8,16},{16,8},{9,17},{17,9},{10,18},{18,10},{11,19},{19,11},{12,20... | collective-permute-start | bytes 393224 | tf_op jit(solution)/shard_map/ppermute | solution.py:648
  20.6 0.1 collective-permute-start.2
  20.7 0.7 %collective-permute-start.3 = (f32[256,128]{1,0:T(8,128)S(1)}, f32[256,128]{1,0:T(8,128)S(1)}, u32[]{:S(2)}, u32[]{:S(2)}) collective-permute-start(f32[256,128]{1,0:T(8,128)S(1)} %get-tuple-element.23), channel_id=1, source_target_pairs={{1,2},{3,4},{5,6},{2,1},{4,3},{6,5},{9,10},{11,12},{13,14},{10,9},... | collective-permute-start | bytes 393224 | tf_op jit(solution)/shard_map/ppermute | solution.py:648
  21.4 4.9 %all-to-all-done = f32[32,8,128]{2,1,0:T(8,128)S(1)} async-done(((f32[32,8,128]{2,1,0:T(8,128)}), f32[32,8,128]{2,1,0:T(8,128)S(1)}, u32[]{:S(2)}, u32[]{:S(2)}) %all-to-all-start) | async-done | bytes 131104 | tf_op jit(solution)/shard_map/all_to_all | solution.py:642
  26.3 2.8 %local_terms.1 = (bf16[432,1024]{1,0:T(8,128)(2,1)S(1)}, f32[48,256]{1,0:T(8,128)S(1)}, bf16[144,256]{1,0:T(8,128)(2,1)S(1)}, s32[1,256]{1,0:T(1,128)S(1)}, s32[...) custom-call(f32[21,4,56]{2,1,0:T(4,128)} %bitcast.14, ...), custom_call_target="tpu_custom_call" | custom-call | flops 905969664 | bytes 8000000 | tf_op jit(solution)/shard_map/local_terms/pallas_call | solution.py:200
  29.1 0.0 collective-permute-done.refs_0_
  29.1 0.0 collective-permute-done.1.refs_1_
  29.2 0.0 collective-permute-done.2.refs_2_
  29.2 0.0 collective-permute-done.3.refs_3_
  29.2 1.6 %friction.1 = (f32[64,128]{1,0:T(8,128)}, f32[24,256]{1,0:T(8,128)S(1)}) custom-call(f32[256,128]{1,0:T(8,128)S(1)} %collective-permute-done.refs_0_, f32[256,128]{1,0:T(8,128)S(1)} %collective-permute-done.1.refs_1_, f32[256,128]{1,0:T(8,128)S(1)} %collective-permute-done.2.refs_2_, f32[256,128]{1,0:T(8,128)S(1)} %collective-permute-done.3.refs_3_, ...), custom_call_target="tpu_custom_call" | custom-call | flops 75497472 | bytes 4000000 | tf_op jit(solution)/shard_map/friction/pallas_call | solution.py:200
  30.8 5.2 %all-to-all-start.1 = ((f32[32,2,128]{2,1,0:T(2,128)}), f32[32,2,128]{2,1,0:T(2,128)S(1)}, u32[]{:S(2)}, u32[]{:S(2)}) async-start(f32[32,2,128]{2,1,0:T(2,128)} %bitcast.6), calls=%async_computation.1 | async-start | bytes 65536 | tf_op jit(solution)/shard_map/all_to_all | solution.py:697
  36.0 6.6 %final_terms.1 = f32[504,256]{1,0:T(8,128)} custom-call(f32[256,128]{1,0:T(8,128)S(1)} %collective-permute-done.refs_0_, f32[256,128]{1,0:T(8,128)S(1)} %collective-permute-done.1.refs_1_, f32[256,128]{1,0:T(8,128)S(1)} %collective-permute-done.2.refs_2_, f32[256,128]{1,0:T(8,128)S(1)} %collective-permute-done.3.refs_3_, ...), custom_call_target="tpu_custom_call" | custom-call | flops 905969664 | bytes 8000000 | tf_op jit(solution)/shard_map/final_terms/pallas_call | solution.py:200
  42.6 0.6 %all-to-all-done.1 = f32[32,2,128]{2,1,0:T(2,128)S(1)} async-done(((f32[32,2,128]{2,1,0:T(2,128)}), f32[32,2,128]{2,1,0:T(2,128)S(1)}, u32[]{:S(2)}, u32[]{:S(2)}) %all-to-all-start.1) | async-done | bytes 32800 | tf_op jit(solution)/shard_map/all_to_all | solution.py:697
  43.2 0.9 %fault_return.1 = f32[21,128]{1,0:T(8,128)} custom-call(s32[1,128]{1,0:T(1,128)S(1)} %get-tuple-element.36.refs_0_, f32[64,128]{1,0:T(8,128)S(1)} %bitcast.11), custom_call_target="tpu_custom_call" | custom-call | flops 3145728 | bytes 200000 | tf_op jit(solution)/shard_map/fault_return/pallas_call | solution.py:200
Async XLA Ops:
  10.8 15.5 %all-to-all-start = ((f32[32,8,128]{2,1,0:T(8,128)}), f32[32,8,128]{2,1,0:T(8,128)S(1)}, u32[]{:S(2)}, u32[]{:S(2)}) async-start(f32[32,8,128]{2,1,0:T(8,128)} %bitcast.12), calls=%async_computation | async-start | bytes 262144 | tf_op jit(solution)/shard_map/all_to_all | solution.py:642
  18.1 11.0 %collective-permute-start = (f32[256,128]{1,0:T(8,128)S(1)}, f32[256,128]{1,0:T(8,128)S(1)}, u32[]{:S(2)}, u32[]{:S(2)}) collective-permute-start(f32[256,128]{1,0:T(8,128)S(1)} %get-tuple-element.20), channel_id=1, source_target_pairs={{0,8},{16,24},{8,0},{24,16},{1,9},{17,25},{9,1},{25,17},{2,10},{18... | collective-permute-start | bytes 393224 | tf_op jit(solution)/shard_map/ppermute | solution.py:648
  20.0 9.2 %collective-permute-start.1 = (f32[256,128]{1,0:T(8,128)S(1)}, f32[256,128]{1,0:T(8,128)S(1)}, u32[]{:S(2)}, u32[]{:S(2)}) collective-permute-start(f32[256,128]{1,0:T(8,128)S(1)} %get-tuple-element.21), channel_id=1, source_target_pairs={{8,16},{16,8},{9,17},{17,9},{10,18},{18,10},{11,19},{19,11},{12,20... | collective-permute-start | bytes 393224 | tf_op jit(solution)/shard_map/ppermute | solution.py:648
  20.6 8.5 %collective-permute-start.2 = (f32[256,128]{1,0:T(8,128)S(1)}, f32[256,128]{1,0:T(8,128)S(1)}, u32[]{:S(2)}, u32[]{:S(2)}) collective-permute-start(f32[256,128]{1,0:T(8,128)S(1)} %get-tuple-element.22), channel_id=1, source_target_pairs={{0,1},{2,3},{4,5},{6,7},{1,0},{3,2},{5,4},{7,6},{8,9},{10,11},{12,... | collective-permute-start | bytes 393224 | tf_op jit(solution)/shard_map/ppermute | solution.py:648
  20.7 8.4 %collective-permute-start.3 = (f32[256,128]{1,0:T(8,128)S(1)}, f32[256,128]{1,0:T(8,128)S(1)}, u32[]{:S(2)}, u32[]{:S(2)}) collective-permute-start(f32[256,128]{1,0:T(8,128)S(1)} %get-tuple-element.23), channel_id=1, source_target_pairs={{1,2},{3,4},{5,6},{2,1},{4,3},{6,5},{9,10},{11,12},{13,14},{10,9},... | collective-permute-start | bytes 393224 | tf_op jit(solution)/shard_map/ppermute | solution.py:648
  30.8 12.4 %all-to-all-start.1 = ((f32[32,2,128]{2,1,0:T(2,128)}), f32[32,2,128]{2,1,0:T(2,128)S(1)}, u32[]{:S(2)}, u32[]{:S(2)}) async-start(f32[32,2,128]{2,1,0:T(2,128)} %bitcast.6), calls=%async_computation.1 | async-start | bytes 65536 | tf_op jit(solution)/shard_map/all_to_all | solution.py:697
